TPU v7x, 512 devices: a whole 4x8x8 slice. The times are simulated.
512 devices in a mesh: row: 16 (over z_hi, x), col: 32 (over z_lo, y, core).
Axes of the slice: x: 4, y: 8, z: 8 (z_hi: 4, z_lo: 2; z = z_hi * 2 + z_lo), core: 2. Of those that a mesh axis runs over, the one named last changes fastest.
Arguments:
- pair: bfloat16 [768, 768, 128], P('row', 'col'), may hold values from -6 to 6
- pair_mask: int32 [768, 768], P('row', 'col'), may hold values 0 or 1
- in_gain: float32 [128], replicated, may hold values from 0.1 to 1.9
- in_bias: float32 [128], replicated, may hold values from -2.5 to 2.5
- proj_weight: bfloat16 [128, 512], replicated, may hold values from -0.5 to 0.5
- gate_weight: bfloat16 [128, 128], replicated, may hold values from -0.5 to 0.5
- out_gain: float32 [128], replicated, may hold values from 0.1 to 1.9
- out_bias: float32 [128], replicated, may hold values from -2.5 to 2.5
- out_weight: bfloat16 [128, 128], replicated, may hold values from -0.5 to 0.5
Outputs:
- update: bfloat16 [768, 768, 128], P('row', 'col')
All inputs are finite; a program needn't handle non-finite values. No bound on the sum of `pair_mask` on one device may be relied on, other than what follows from the above.
Results may differ from a plain program's by a relative error of at most 0.0052.
Values may be sent and summed in bfloat16 or wider, within the bound.
No kernel may reach another device: no remote copies, remote signals or barrier semaphores. Data moves between devices by JAX's collectives and lax.ppermute only.
A program may use at most 128 MiB of HBM per device.

v0:
```python
import jax
import jax.numpy as jnp
from jax import lax
from jax.sharding import PartitionSpec as P


def spread(value, axis, source):
    kept = jnp.where(lax.axis_index(axis) == source, value, 0).astype(value.dtype)
    return lax.psum(kept, axis)


def layer_norm(values, gain, bias):
    values = values.astype(jnp.float32)
    mean = jnp.mean(values, axis=-1, keepdims=True)
    centred = values - mean
    var = jnp.mean(centred * centred, axis=-1, keepdims=True)
    return centred * lax.rsqrt(var + 1e-05) * gain + bias


def factor(normed, weight, mask_values):
    width = normed.shape[-1]
    flat = normed.reshape(-1, width)
    hidden = jnp.dot(flat, weight, preferred_element_type=jnp.float32)
    hidden = hidden.reshape(normed.shape[:-1] + (2 * width,))
    result = jax.nn.sigmoid(hidden[..., width:]) * hidden[..., :width]
    return (result * mask_values[..., None]).astype(jnp.bfloat16)


def per_device(
    pair, pair_mask, in_gain, in_bias, proj_weight, gate_weight, out_gain, out_bias, out_weight
):
    row_count, col_count, width = pair.shape
    mask_values = pair_mask.astype(jnp.float32)
    normed = layer_norm(pair, in_gain, in_bias).astype(jnp.bfloat16)
    left_tile = factor(normed, proj_weight[:, : 2 * width], mask_values)
    right_tile = factor(normed, proj_weight[:, 2 * width :], mask_values)
    gate = jax.nn.sigmoid(
        jnp.dot(normed.reshape(-1, width), gate_weight, preferred_element_type=jnp.float32)
    )
    col_index = lax.axis_index("col")
    ratio = lax.axis_size("col") // lax.axis_size("row")
    root = col_index // ratio
    offset = col_index % ratio * col_count
    left, band_rows = (
        lax.all_gather(left_tile, "col", axis=1, tiled=True),
        lax.all_gather(right_tile, "col", axis=1, tiled=True),
    )
    part_right = lax.dynamic_slice_in_dim(band_rows, offset, col_count, 0)
    right = spread(part_right, "row", root)
    combined = jnp.einsum("ikc,jkc->ijc", left, right, preferred_element_type=jnp.float32)
    onorm = layer_norm(combined, out_gain, out_bias).astype(jnp.bfloat16)
    projected = jnp.dot(onorm.reshape(-1, width), out_weight, preferred_element_type=jnp.float32)
    return (gate * projected).reshape(row_count, col_count, width).astype(jnp.bfloat16)


def solution(mesh):
    return jax.shard_map(
        per_device,
        mesh=mesh,
        in_specs=(P("row", "col", None), P("row", "col"), P(), P(), P(), P(), P(), P(), P()),
        out_specs=P("row", "col", None),
        check_vma=False,
    )
```

profile of v0, /device:TPU:1, one launch (start us, length us, event | category | flops | bytes accessed | tf_op | source)
XLA Modules:
  0.0 450.8 jit_solution(7415786697954929952)
XLA Ops:
  6.5 0.0 copy-start
  6.5 0.0 copy-start.1
  6.5 0.0 all-gather.3.cloned.1.call-start
  6.5 1.2 convert_reduce_fusion
  7.8 0.1 copy.35
  7.8 0.1 copy.36
  7.9 1.4 fusion.6
  9.3 0.1 copy.37
  9.4 0.1 copy.38
  9.5 1.4 fusion.9
  10.8 0.0 copy-start.3
  10.8 1.1 fusion.20
  12.0 0.0 copy-done.1
  12.0 0.3 fusion.22
  12.3 0.0 copy-done.3
  12.3 0.1 copy.39
  12.4 1.2 fusion.11
  13.6 0.0 all-gather.3.cloned.1.call-update
  13.6 0.0 all-gather.5.cloned.1.call-start
  13.6 0.7 all-gather.5.cloned.1.call-update
  14.3 0.0 all-reduce.2.cloned.1.call-start
  14.4 82.6 %all-gather.3.cloned.1.call-done = bf16[48,768,128]{2,1,0:T(8,128)(2,1)} async-done(((bf16[48,24,128]{2,1,0:T(8,128)(2,1)}), bf16[48,768,128]{2,1,0:T(8,128)(2,1)}) %all-gather.3.cloned.1.call-update) | async-done | bytes 9437200 | tf_op jit(solution)/shard_map/all_gather | solution.py:46
  97.0 4.8 %dynamic-slice_select_fusion = bf16[24,768,128]{2,1,0:T(8,128)(2,1)} fusion(bf16[48,768,128]{2,1,0:T(8,128)(2,1)} %all-gather.3.cloned.1.call-done, s32[]{:T(128)S(6)} %select_n.25, pred[]{:T(512)S(6)} %eq.5), kind=kLoop, calls=%fused_computation | loop fusion | flops 2359296 | bytes 9437189 | tf_op jit(solution)/shard_map/jit(_where)/select_n | solution.py:8
  101.8 0.0 all-reduce.2.cloned.1.call-update
  101.8 0.0 copy-done
  101.8 0.3 fusion.2
  102.2 73.5 %all-gather.5.cloned.1.call-done = bf16[48,768,128]{2,1,0:T(8,128)(2,1)} async-done(((bf16[48,24,128]{2,1,0:T(8,128)(2,1)}), bf16[48,768,128]{2,1,0:T(8,128)(2,1)}) %all-gather.5.cloned.1.call-update) | async-done | bytes 9437200 | tf_op jit(solution)/shard_map/all_gather | solution.py:45
  175.6 42.2 %copy.41 = bf16[48,768,128]{0,1,2:T(8,128)(2,1)} copy(bf16[48,768,128]{2,1,0:T(8,128)(2,1)} %all-gather.5.cloned.1.call-done) | data formatting | bytes 18874368 | tf_op jit(solution)/shard_map/all_gather | solution.py:45
  217.9 204.9 %all-reduce.2.cloned.1.call-done = bf16[24,768,128]{2,1,0:T(8,128)(2,1)} async-done(((bf16[24,768,128]{2,1,0:T(8,128)(2,1)}), bf16[24,768,128]{2,1,0:T(8,128)(2,1)}) %all-reduce.2.cloned.1.call-update) | async-done | bytes 4718608 | tf_op jit(solution)/shard_map/psum | solution.py:9
  422.8 7.1 %copy.40 = bf16[24,768,128]{1,0,2:T(8,128)(2,1)} copy(bf16[24,768,128]{2,1,0:T(8,128)(2,1)} %all-reduce.2.cloned.1.call-done) | data formatting | bytes 9437184 | tf_op jit(solution)/shard_map/psum | solution.py:9
  429.9 11.8 %bitcast_reduce_fusion = (f32[48,24]{0,1:T(8,128)S(1)}, f32[128,24,48]{2,1,0:T(8,128)S(1)}) fusion(bf16[24,768,128]{1,0,2:T(8,128)(2,1)} %copy.40, bf16[48,768,128]{0,1,2:T(8,128)(2,1)} %copy.41), kind=kOutput, calls=%fused_computation.8 | convolution fusion | flops 226638720 | bytes 14750208 | tf_op jit(solution)/shard_map/ikc,jkc->ijc/dot_general | solution.py:50
  441.7 0.0 copy-start.4
  441.8 0.0 copy-start.5
  441.8 0.3 multiply_reduce_fusion
  442.1 0.3 copy-done.4
  442.4 0.0 copy-done.5
  442.4 0.0 copy-start.2
  442.4 0.3 add_convert_fusion
  442.8 0.5 copy.42
  443.3 0.0 copy-done.2
  443.3 0.9 fusion.3
  (5 shorter events, 0.0 us)
Async XLA Ops:
  6.5 95.3 %copy-start = (bf16[128,128]{1,0:T(8,128)(2,1)S(1)}, bf16[128,128]{1,0:T(8,128)(2,1)}, u32[]{:S(2)}) copy-start(bf16[128,128]{1,0:T(8,128)(2,1)} %param.14) | copy-start | bytes 98308
  6.5 5.4 %copy-start.1 = (bf16[128,512]{1,0:T(8,128)(2,1)S(1)}, bf16[128,512]{1,0:T(8,128)(2,1)}, u32[]{:S(2)}) copy-start(bf16[128,512]{1,0:T(8,128)(2,1)} %param.13) | copy-start | bytes 393220
  6.5 90.5 %all-gather.3.cloned.1.call-start = ((), (), s32[]{:S(2)}) async-start(), calls=%async_computation | async-start | bytes 9732096 | tf_op jit(solution)/shard_map/all_gather | solution.py:46
  10.8 1.5 copy-start.3
  13.6 162.0 %all-gather.5.cloned.1.call-start = ((), (), s32[]{:S(2)}) async-start(), calls=%async_computation.2 | async-start | bytes 9732096 | tf_op jit(solution)/shard_map/all_gather | solution.py:45
  14.3 408.5 %all-reduce.2.cloned.1.call-start = ((), (), s32[]{:S(2)}) async-start(), calls=%async_computation.1 | async-start | bytes 9437184 | tf_op jit(solution)/shard_map/psum | solution.py:9
  441.7 0.7 copy-start.4
  441.8 0.7 copy-start.5
  442.4 0.9 copy-start.2
Sparse Core Ops, SparseCore 0:
  13.7 83.2 all-gather.2
  99.1 76.4 all-gather.4
  178.6 244.1 all-reduce.1
where the time goes:
time: 452 us; the launch traced here: 451 us
  waiting for transfers between devices  362 us (80%)
  local copies, waits for them, and re-layouts  50.7 us (11%)
  matrix products  14.5 us (3%)
  between operations  13.3 us (3%)
  other arithmetic  10.5 us (2%)
    psum x1, waiting for transfers between devices, spread(): return lax.psum(kept, axis)  205 us
    all_gather x1, waiting for transfers between devices, per_device(): lax.all_gather(right_tile, 'col', axis=1, tiled=True)  82.6 us
    all_gather x1, waiting for transfers between devices, per_device(): lax.all_gather(left_tile, 'col', axis=1, tiled=True)  73.5 us
    all_gather x1, local copies, waits for them, and re-layouts, per_device(): lax.all_gather(left_tile, 'col', axis=1, tiled=True)  42.2 us
    dot_general x1, matrix products, per_device(): jnp.einsum('ikc,jkc->ijc', left, right, preferred_element_type=jnp.float32)  11.8 us
  transfers between devices with their start and end apart: 3, of which 3 were waited for; matrix products, arithmetic and copies ran while one was open for 10% of the time, Pallas kernels for 0%

commit v1 on v0

v1 whole, which is shorter than its diff:
```python
import functools

import jax
import jax.numpy as jnp
from jax import lax
from jax.experimental import pallas as pl
from jax.experimental.pallas import tpu as pltpu
from jax.sharding import PartitionSpec as P

BF16 = jnp.bfloat16
F32 = jnp.float32
AXES = ("row", "col")
ROWS, COLS, WIDTH = 48, 24, 128
HALF = COLS // 2
SPAN = HALF * ROWS
RPOS, QPOS = 8, 16
LANES = 128
SIDE = RPOS * ROWS
JSPAN = RPOS * COLS


def sigmoid(x):
    return 0.5 * jnp.tanh(0.5 * x) + 0.5


def device(z_hi, x, z_lo, y, core):
    return (z_hi * 4 + x) * 32 + z_lo * 16 + y * 2 + core


def x_of(side, x_low):
    return x_low if side == 0 else 3 - x_low


def positions():
    return [(zh, xl, zl, y) for zh in range(4) for xl in range(2) for zl in range(2) for y in range(8)]


def channel_groups():
    return [
        [device(zh, x_of(side, xl), zl, y, core) for zh, xl, zl, y in positions()]
        for side in range(2)
        for core in range(2)
    ]


def quad_groups():
    return [
        [device(zh, x_of(side, xl), zl, y, core) for side in range(2) for core in range(2)]
        for zh, xl, zl, y in positions()
    ]


def core_swap():
    return [(d, d ^ 1) for d in range(512)]


def dot(a, b, dims):
    return lax.dot_general(a, b, (dims, ((), ())), preferred_element_type=F32)


def call(kernel, out_shape, scratch=(), name=None):
    return pl.pallas_call(
        kernel,
        out_shape=out_shape,
        scratch_shapes=list(scratch),
        compiler_params=pltpu.CompilerParams(vmem_limit_bytes=16 * 2**20),
        name=name,
    )


def factors_kernel(x_ref, mask_ref, gain_ref, bias_ref, w_ref, send_ref, normed_ref, tokens, pairs):
    tokens[...] = x_ref[...].astype(F32)
    values = jnp.concatenate([tokens[pl.ds(k, ROWS, stride=COLS), :] for k in range(COLS)], axis=0)
    mean = jnp.mean(values, axis=-1, keepdims=True)
    centred = values - mean
    var = jnp.mean(centred * centred, axis=-1, keepdims=True)
    normed = (centred * lax.rsqrt(var + 1e-05) * gain_ref[...] + bias_ref[...]).astype(BF16)
    normed_ref[...] = normed
    token = lax.broadcasted_iota(jnp.int32, (ROWS, ROWS * COLS), 1)
    spread = (lax.rem(token, ROWS) == lax.broadcasted_iota(jnp.int32, token.shape, 0)).astype(BF16)
    every = dot(mask_ref[...].astype(F32).astype(BF16), spread, ((1,), (0,)))
    token = lax.broadcasted_iota(jnp.int32, every.shape, 1)
    first = lax.broadcasted_iota(jnp.int32, every.shape, 0) * ROWS
    mask = jnp.sum(jnp.where((token >= first) & (token < first + ROWS), every, 0.0), axis=0, keepdims=True)
    weight = w_ref[...].T
    for half in range(2):
        part = normed[half * SPAN : (half + 1) * SPAN]
        part_mask = mask[:, half * SPAN : (half + 1) * SPAN]
        sides = []
        for side in range(2):
            hidden = dot(weight[side * 2 * WIDTH : (side + 1) * 2 * WIDTH], part, ((1,), (1,)))
            sides.append(sigmoid(hidden[WIDTH:]) * hidden[:WIDTH] * part_mask)
        both = jnp.concatenate(sides, axis=1)
        for t in range(2 * SPAN // LANES):
            pairs[t, pl.ds(half, WIDTH, stride=2), :] = both[:, t * LANES : (t + 1) * LANES]
    for t in range(2 * SPAN // LANES):
        send_ref[:, :, t * LANES : (t + 1) * LANES] = pairs[t].astype(BF16).reshape(WIDTH, 2, LANES)


def gate_kernel(normed_ref, w_ref, gate_ref):
    gate_ref[...] = sigmoid(dot(normed_ref[...], w_ref[...], ((1,), (0,))))


def right_kernel(x_ref, out_ref):
    x = x_ref[...].reshape(RPOS * QPOS * 2, 2 * SPAN)[:, SPAN:]
    rows = 2 * QPOS
    for b in range(2):
        for k in range(HALF // 2):
            block = jnp.concatenate(
                [
                    x[rp * rows : (rp + 1) * rows, (h * 6 + k) * ROWS + b * COLS : (h * 6 + k) * ROWS + (b + 1) * COLS]
                    for h in range(2)
                    for rp in range(RPOS)
                ],
                axis=1,
            )
            out_ref[b, k * rows : (k + 1) * rows, :] = block
            out_ref[2 + b, k * rows : (k + 1) * rows, :] = block


def left_kernel(x_ref, out_ref):
    x = x_ref[...].reshape(RPOS * QPOS * 2, 2 * SPAN)[:, :SPAN]
    rows = 2 * QPOS
    for k in range(HALF):
        out_ref[k * rows : (k + 1) * rows, :] = jnp.concatenate(
            [x[rp * rows : (rp + 1) * rows, k * ROWS : (k + 1) * ROWS] for rp in range(RPOS)], axis=1
        )


def contract_kernel(own_ref, other_ref, right_ref, core_ref, send_ref, total):
    core = core_ref[0]
    own, other = own_ref[...], other_ref[...]
    left = [jnp.where(core == b, own, other) for b in range(2)]
    for side in range(2):
        part = jnp.zeros((JSPAN, SIDE), F32)
        for b in range(2):
            right = right_ref[side * 2 + b]
            for h in range(2):
                part += dot(right[:, h * JSPAN : (h + 1) * JSPAN], left[b][h * JSPAN : (h + 1) * JSPAN], ((0,), (0,)))
        for rp in range(RPOS):
            row = (rp // 2) * 4 + x_of(side, rp % 2)
            for t in range(SIDE // LANES):
                total[t, row * COLS : (row + 1) * COLS, :] = part[rp * COLS : (rp + 1) * COLS, t * LANES : (t + 1) * LANES]
    rows = 2 * QPOS
    blocks = [
        jnp.concatenate([total[t, pl.ds(j, rows, stride=HALF), :] for t in range(SIDE // LANES)], axis=1)
        for j in range(HALF)
    ]
    for rp in range(RPOS):
        piece = jnp.concatenate([block[:, rp * ROWS : (rp + 1) * ROWS] for block in blocks], axis=1)
        send_ref[rp * QPOS : (rp + 1) * QPOS] = piece.astype(BF16).reshape(QPOS, 2, SPAN)


def update_kernel(x_ref, gate_ref, gain_ref, bias_ref, w_ref, out_ref, pairs, tokens):
    arrived = x_ref[...].reshape(2 * WIDTH, SPAN).astype(F32)
    tiles = pl.cdiv(SPAN, LANES)
    for t in range(tiles):
        tile = arrived[:, t * LANES : (t + 1) * LANES]
        pairs[t, :, : tile.shape[1]] = tile
    for half in range(2):
        values = [pairs[t, pl.ds(half, WIDTH, stride=2), :] for t in range(tiles)]
        values = jnp.concatenate(values, axis=1)[:, :SPAN]
        mean = jnp.mean(values, axis=0, keepdims=True)
        centred = values - mean
        var = jnp.mean(centred * centred, axis=0, keepdims=True)
        onorm = (centred * lax.rsqrt(var + 1e-05) * gain_ref[...] + bias_ref[...]).astype(BF16)
        update = dot(onorm, w_ref[...], ((0,), (0,))) * gate_ref[half * SPAN : (half + 1) * SPAN]
        for j in range(HALF):
            tokens[pl.ds(half * HALF + j, ROWS, stride=COLS), :] = update[j * ROWS : (j + 1) * ROWS]
    out_ref[...] = tokens[...].astype(BF16)


def per_device(
    pair, pair_mask, in_gain, in_bias, proj_weight, gate_weight, out_gain, out_bias, out_weight
):
    shape = jax.ShapeDtypeStruct
    count = ROWS * COLS
    send, normed = call(
        factors_kernel,
        (shape((WIDTH, 2, 2 * SPAN), BF16), shape((count, WIDTH), BF16)),
        (pltpu.VMEM((count, WIDTH), F32), pltpu.VMEM((2 * SPAN // LANES, 2 * WIDTH, LANES), F32)),
        "factors",
    )(pair.reshape(count, WIDTH), pair_mask.T, in_gain[None], in_bias[None], proj_weight)
    exchange = functools.partial(
        lax.all_to_all, axis_name=AXES, split_axis=0, concat_axis=0, axis_index_groups=channel_groups(), tiled=True
    )
    both = exchange(send)
    gate = call(gate_kernel, shape((count, WIDTH), F32), name="gate")(normed, gate_weight)
    right = call(right_kernel, shape((4, JSPAN, SIDE), BF16), name="right")(both)
    right = lax.all_to_all(right, AXES, 0, 0, axis_index_groups=quad_groups(), tiled=True)
    left = call(left_kernel, shape((SIDE, SIDE), BF16), name="left")(both)
    other = lax.ppermute(left, AXES, core_swap())
    core = lax.rem(lax.axis_index("col"), 2).astype(jnp.int32).reshape(1)
    combined = pl.pallas_call(
        contract_kernel,
        out_shape=shape((RPOS * QPOS, 2, SPAN), BF16),
        in_specs=[pl.BlockSpec(memory_space=pltpu.VMEM)] * 3 + [pl.BlockSpec(memory_space=pltpu.SMEM)],
        scratch_shapes=[pltpu.VMEM((SIDE // LANES, SIDE, LANES), F32)],
        compiler_params=pltpu.CompilerParams(vmem_limit_bytes=16 * 2**20),
        name="contract",
    )(left, other, right, core)
    combined = exchange(combined)
    update = call(
        update_kernel,
        shape((count, WIDTH), BF16),
        (pltpu.VMEM((pl.cdiv(SPAN, LANES), 2 * WIDTH, LANES), F32), pltpu.VMEM((count, WIDTH), F32)),
        "update",
    )(combined, gate, out_gain[:, None], out_bias[:, None], out_weight)
    return update.reshape(ROWS, COLS, WIDTH)


def solution(mesh):
    return jax.shard_map(
        per_device,
        mesh=mesh,
        in_specs=(P("row", "col", None), P("row", "col"), P(), P(), P(), P(), P(), P(), P()),
        out_specs=P("row", "col", None),
        check_vma=False,
    )
```

time: 452 us -> 84.8 us (0.19)
  waiting for transfers between devices: 362 us -> 19 us
  local copies, waits for them, and re-layouts: 50.7 us -> 5.42 us
  blocking collectives: 0 us -> 38.3 us
  matrix products: 14.5 us -> 0 us
  starting transfers between devices: 0.08 us -> 14.3 us
  between operations: 13.3 us -> 0.07 us
  other arithmetic: 10.5 us -> 0 us
  Pallas kernels: 0 us -> 6.4 us
    psum x1 -> x0, waiting for transfers between devices: 205 us -> none  [spread(): return lax.psum(kept, axis)]
    all_gather x2 -> x0, waiting for transfers between devices: 156 us -> none  [the longest x1 82.6 us: per_device(): lax.all_gather(right_tile, 'col', axis=1, tiled=True)]
    all_gather x1 -> x0, local copies, waits for them, and re-layouts: 42.2 us -> none  [per_device(): lax.all_gather(left_tile, 'col', axis=1, tiled=True)]
    all_to_all x0 -> x1, blocking collectives: none -> 38.3 us  [per_device(): both = exchange(send)]
    all_to_all x0 -> x2, waiting for transfers between devices: none -> 17.4 us  [the longest x1 11.3 us: per_device(): combined = exchange(combined)]
    dot_general x5 -> x0, matrix products: 14.5 us -> none  [the longest x1 11.8 us: per_device(): jnp.einsum('ikc,jkc->ijc', left, right, preferred_element_type=jnp.float32)]
    all_to_all x0 -> x2, starting transfers between devices: none -> 12.3 us  [the longest x1 6.29 us: per_device(): combined = exchange(combined)]
    psum x1 -> x0, local copies, waits for them, and re-layouts: 7.14 us -> none  [spread(): return lax.psum(kept, axis)]
  transfers between devices with their start and end apart: 3 -> 3, of which waited for: 3 -> 3; matrix products, arithmetic and copies ran while one was open for 10% -> 0% of each run, Pallas kernels for 0% -> 1%
where the time goes in v1:
time: 84.8 us; the launch traced here: 83.5 us
  blocking collectives  38.3 us (45%)
  waiting for transfers between devices  19 us (22%)
  starting transfers between devices  14.3 us (17%)
  Pallas kernels  6.4 us (8%)
  local copies, waits for them, and re-layouts  5.42 us (6%)
    all_to_all x1, blocking collectives, per_device(): both = exchange(send)  38.3 us
    all_to_all x1, waiting for transfers between devices, per_device(): combined = exchange(combined)  11.3 us
    all_to_all x1, starting transfers between devices, per_device(): combined = exchange(combined)  6.29 us
    all_to_all x1, waiting for transfers between devices, per_device(): lax.all_to_all(right, AXES, 0, 0, axis_index_groups=quad_groups(), tiled=...  6.1 us
    all_to_all x1, starting transfers between devices, per_device(): lax.all_to_all(right, AXES, 0, 0, axis_index_groups=quad_groups(), tiled=...  6.05 us
    unnamed x18, local copies, waits for them, and re-layouts  5.19 us
    ppermute x1, starting transfers between devices, per_device(): other = lax.ppermute(left, AXES, core_swap())  1.95 us
    pallas_call x1, Pallas kernels, per_device(): pl.pallas_call(contract_kernel, out_shape=shape((RPOS * QPOS, 2, SPAN), B...  1.79 us
  transfers between devices with their start and end apart: 3, of which 3 were waited for; matrix products, arithmetic and copies ran while one was open for 0% of the time, Pallas kernels for 1%

profile of v1, /device:TPU:1, one launch (start us, length us, event | category | flops | bytes accessed | tf_op | source)
XLA Modules:
  0.0 83.5 jit_solution(14336328275936589486)
XLA Ops:
  0.0 0.0 copy-start.5
  0.0 0.0 copy-start.6
  0.0 0.7 copy-done.5
  0.7 0.0 copy-done.6
  0.7 0.0 copy-start
  0.7 1.0 %copy-done = bf16[48,24,128]{2,1,0:T(8,128)(2,1)S(1)} copy-done((bf16[48,24,128]{2,1,0:T(8,128)(2,1)S(1)}, bf16[48,24,128]{2,1,0:T(8,128)(2,1)}, u32[]{:S(2)}) %copy-start) | copy-done | bytes 294936
  1.6 0.0 copy-start.1
  1.6 0.9 %copy-done.1 = bf16[128,512]{1,0:T(8,128)(2,1)S(1)} copy-done((bf16[128,512]{1,0:T(8,128)(2,1)S(1)}, bf16[128,512]{1,0:T(8,128)(2,1)}, u32[]{:S(2)}) %copy-start.1) | copy-done | bytes 131096
  2.5 0.0 copy-start.4
  2.5 0.7 copy-done.4
  3.2 1.3 %factors.1 = (bf16[128,2,1152]{2,1,0:T(2,128)(2,1)S(1)}, bf16[1152,128]{1,0:T(8,128)(2,1)S(1)}) custom-call(bf16[1152,128]{1,0:T(8,128)(2,1)S(1)} %bitcast.8, s32[24,48]{1,0:T(8,128)S(1)} %bitcast.9, f32[1,128]{1,0:T(1,128)S(1)} %bitcast.10, f32[1,128]{1,0:T(1,128)S(1)} %bitcast.11, bf16[128,512]{1,0:T(8,128)(2,1)S(1)} %copy-done.1), custom_call_target="tpu_custom_call" | custom-call | tf_op jit(solution)/shard_map/factors/pallas_call | solution.py:178
  4.6 38.3 %all_to_all.15.x_ref = bf16[128,2,1152]{2,1,0:T(2,128)(2,1)S(1)} all-to-all(bf16[128,2,1152]{2,1,0:T(2,128)(2,1)S(1)} %get-tuple-element.7), channel_id=1, replica_groups={{0,2,4,6,8,10,12,14,16,18,20,22,24,26,28,30,32,34,36,38,40,42,44,46,48,..., dimensions={0} | all-to-all | bytes 1179648 | tf_op jit(solution)/shard_map/all_to_all | solution.py:187
  42.9 1.3 %right.1 = bf16[4,192,384]{2,1,0:T(8,128)(2,1)} custom-call(bf16[128,2,1152]{2,1,0:T(2,128)(2,1)S(1)} %all_to_all.15.x_ref), custom_call_target="tpu_custom_call" | custom-call | tf_op jit(solution)/shard_map/right/pallas_call | solution.py:189
  44.2 6.0 %all-to-all-start.1 = ((bf16[4,192,384]{2,1,0:T(8,128)(2,1)}), bf16[4,192,384]{2,1,0:T(8,128)(2,1)S(1)}, u32[]{:S(2)}, u32[]{:S(2)}) async-start(bf16[4,192,384]{2,1,0:T(8,128)(2,1)} %right.1), calls=%async_computation.1 | async-start | bytes 1179648 | tf_op jit(solution)/shard_map/all_to_all | solution.py:190
  50.3 0.3 left.1.own_ref
  50.6 1.9 %collective-permute-start = (bf16[384,384]{1,0:T(8,128)(2,1)S(1)}, bf16[384,384]{1,0:T(8,128)(2,1)S(1)}, u32[]{:S(2)}, u32[]{:S(2)}) collective-permute-start(bf16[384,384]{1,0:T(8,128)(2,1)S(1)} %left.1.own_ref), channel_id=1, source_target_pairs={{0,1},{1,0},{2,3},{3,2},{4,5},{5,4},{6,7},{7,6},{8,9},{9,8},{10,11... | collective-permute-start | bytes 884744 | tf_op jit(solution)/shard_map/ppermute | solution.py:192
  52.6 1.5 %collective-permute-done.other_ref = bf16[384,384]{1,0:T(8,128)(2,1)S(1)} collective-permute-done((bf16[384,384]{1,0:T(8,128)(2,1)S(1)}, bf16[384,384]{1,0:T(8,128)(2,1)S(1)}, u32[]{:S(2)}, u32[]{:S(2)}) %collective-permute-start) | collective-permute-done | bytes 294944 | tf_op jit(solution)/shard_map/ppermute | solution.py:192
  54.1 6.1 %all-to-all-done.1.right_ref = bf16[4,192,384]{2,1,0:T(8,128)(2,1)S(1)} async-done(((bf16[4,192,384]{2,1,0:T(8,128)(2,1)}), bf16[4,192,384]{2,1,0:T(8,128)(2,1)S(1)}, u32[]{:S(2)}, u32[]{:S(2)}) %all-to-all-start.1) | async-done | bytes 589856 | tf_op jit(solution)/shard_map/all_to_all | solution.py:190
  60.2 1.8 %contract.1 = bf16[128,2,576]{2,1,0:T(2,128)(2,1)} custom-call(bf16[384,384]{1,0:T(8,128)(2,1)S(1)} %left.1.own_ref, bf16[384,384]{1,0:T(8,128)(2,1)S(1)} %collective-permute-done.other_ref, bf16[4,192,384]{2,1,0:T(8,128)(2,1)S(1)} %all-to-all-done.1.right_ref, s32[1]{0:T(128)} %bitcast.4.core_ref), custom_call_target="tpu_custom_call" | custom-call | tf_op jit(solution)/shard_map/contract/pallas_call | solution.py:194
  62.0 6.3 %all-to-all-start.2 = ((bf16[128,2,576]{2,1,0:T(2,128)(2,1)}), bf16[128,2,576]{2,1,0:T(2,128)(2,1)S(1)}, u32[]{:S(2)}, u32[]{:S(2)}) async-start(bf16[128,2,576]{2,1,0:T(2,128)(2,1)} %contract.1), calls=%async_computation.2 | async-start | bytes 655360 | tf_op jit(solution)/shard_map/all_to_all | solution.py:202
  68.3 0.0 copy-start.7
  68.3 0.6 copy-done.7
  68.9 0.1 copy.10.gain_ref
  69.0 0.0 copy-start.8
  69.0 0.7 copy-done.8
  69.7 0.0 copy-start.2
  69.7 0.1 copy.11.bias_ref
  69.8 0.6 copy-done.2
  70.5 0.0 copy-start.3
  70.5 0.2 gate.1.gate_ref
  70.7 11.3 %all-to-all-done.2.x_ref = bf16[128,2,576]{2,1,0:T(2,128)(2,1)S(1)} async-done(((bf16[128,2,576]{2,1,0:T(2,128)(2,1)}), bf16[128,2,576]{2,1,0:T(2,128)(2,1)S(1)}, u32[]{:S(2)}, u32[]{:S(2)}) %all-to-all-start.2) | async-done | bytes 294944 | tf_op jit(solution)/shard_map/all_to_all | solution.py:202
  82.0 0.0 copy-done.3
  82.0 1.4 %update.1 = bf16[1152,128]{1,0:T(8,128)(2,1)} custom-call(bf16[128,2,576]{2,1,0:T(2,128)(2,1)S(1)} %all-to-all-done.2.x_ref, f32[1152,128]{1,0:T(8,128)S(1)} %gate.1.gate_ref, f32[128,1]{1,0:T(8,128)S(1)} %copy.10.gain_ref, f32[128,1]{1,0:T(8,128)S(1)} %copy.11.bias_ref, bf16[128,128]{1,0:T(8,128)(2,1)S(1)} %copy-done.3), custom_call_target="tpu_custom_call" | custom-call | tf_op jit(solution)/shard_map/update/pallas_call | solution.py:203
Async XLA Ops:
  0.0 0.7 copy-start.5
  0.0 0.7 copy-start.6
  0.7 1.0 %copy-start = (bf16[48,24,128]{2,1,0:T(8,128)(2,1)S(1)}, bf16[48,24,128]{2,1,0:T(8,128)(2,1)}, u32[]{:S(2)}) copy-start(bf16[48,24,128]{2,1,0:T(8,128)(2,1)} %param.9) | copy-start | bytes 884740
  1.6 0.9 %copy-start.1 = (bf16[128,512]{1,0:T(8,128)(2,1)S(1)}, bf16[128,512]{1,0:T(8,128)(2,1)}, u32[]{:S(2)}) copy-start(bf16[128,512]{1,0:T(8,128)(2,1)} %w_ref.3) | copy-start | bytes 393220
  2.5 0.7 copy-start.4
  44.2 15.9 %all-to-all-start.1 = ((bf16[4,192,384]{2,1,0:T(8,128)(2,1)}), bf16[4,192,384]{2,1,0:T(8,128)(2,1)S(1)}, u32[]{:S(2)}, u32[]{:S(2)}) async-start(bf16[4,192,384]{2,1,0:T(8,128)(2,1)} %right.1), calls=%async_computation.1 | async-start | bytes 1179648 | tf_op jit(solution)/shard_map/all_to_all | solution.py:190
  50.6 3.5 %collective-permute-start = (bf16[384,384]{1,0:T(8,128)(2,1)S(1)}, bf16[384,384]{1,0:T(8,128)(2,1)S(1)}, u32[]{:S(2)}, u32[]{:S(2)}) collective-permute-start(bf16[384,384]{1,0:T(8,128)(2,1)S(1)} %left.1.own_ref), channel_id=1, source_target_pairs={{0,1},{1,0},{2,3},{3,2},{4,5},{5,4},{6,7},{7,6},{8,9},{9,8},{10,11... | collective-permute-start | bytes 884744 | tf_op jit(solution)/shard_map/ppermute | solution.py:192
  62.0 20.1 %all-to-all-start.2 = ((bf16[128,2,576]{2,1,0:T(2,128)(2,1)}), bf16[128,2,576]{2,1,0:T(2,128)(2,1)S(1)}, u32[]{:S(2)}, u32[]{:S(2)}) async-start(bf16[128,2,576]{2,1,0:T(2,128)(2,1)} %contract.1), calls=%async_computation.2 | async-start | bytes 655360 | tf_op jit(solution)/shard_map/all_to_all | solution.py:202
  68.3 0.7 copy-start.7
  69.0 0.7 copy-start.8
  69.7 0.8 copy-start.2
  70.5 11.6 %copy-start.3 = (bf16[128,128]{1,0:T(8,128)(2,1)S(1)}, bf16[128,128]{1,0:T(8,128)(2,1)}, u32[]{:S(2)}) copy-start(bf16[128,128]{1,0:T(8,128)(2,1)} %w_ref.5) | copy-start | bytes 98308

commit v2 on v1

--- a/solution.py
+++ b/solution.py
@@ -11,6 +11,7 @@
 F32 = jnp.float32
 AXES = ("row", "col")
 ROWS, COLS, WIDTH = 48, 24, 128
+WEIGHT = 100
 HALF = COLS // 2
 SPAN = HALF * ROWS
 RPOS, QPOS = 8, 16
@@ -43,15 +44,15 @@
     ]
 
 
-def quad_groups():
+def swap(mirror, core):
     return [
-        [device(zh, x_of(side, xl), zl, y, core) for side in range(2) for core in range(2)]
-        for zh, xl, zl, y in positions()
+        (device(zh, x, zl, y, c), device(zh, 3 - x if mirror else x, zl, y, 1 - c if core else c))
+        for zh in range(4)
+        for x in range(4)
+        for zl in range(2)
+        for y in range(8)
+        for c in range(2)
     ]
-
-
-def core_swap():
-    return [(d, d ^ 1) for d in range(512)]
 
 
 def dot(a, b, dims):
@@ -68,7 +69,15 @@
     )
 
 
-def factors_kernel(x_ref, mask_ref, gain_ref, bias_ref, w_ref, send_ref, normed_ref, tokens, pairs):
+def factors_kernel(*refs):
+    given, (send_ref, normed_ref), held = refs[:5], refs[5:7], refs[7:12]
+    tokens, pairs, sems = refs[12:]
+    copies = [pltpu.make_async_copy(src, dst, sems.at[n]) for n, (src, dst) in enumerate(zip(given, held))]
+    for copy in copies:
+        copy.start()
+    for copy in copies:
+        copy.wait()
+    x_ref, mask_ref, gain_ref, bias_ref, w_ref = held
     tokens[...] = x_ref[...].astype(F32)
     values = jnp.concatenate([tokens[pl.ds(k, ROWS, stride=COLS), :] for k in range(COLS)], axis=0)
     mean = jnp.mean(values, axis=-1, keepdims=True)
@@ -101,12 +110,13 @@
     gate_ref[...] = sigmoid(dot(normed_ref[...], w_ref[...], ((1,), (0,))))
 
 
-def right_kernel(x_ref, out_ref):
+def right_kernel(x_ref, core_ref, keep_ref, send_ref):
     x = x_ref[...].reshape(RPOS * QPOS * 2, 2 * SPAN)[:, SPAN:]
+    core = core_ref[0]
     rows = 2 * QPOS
-    for b in range(2):
-        for k in range(HALF // 2):
-            block = jnp.concatenate(
+    for k in range(HALF // 2):
+        blocks = [
+            jnp.concatenate(
                 [
                     x[rp * rows : (rp + 1) * rows, (h * 6 + k) * ROWS + b * COLS : (h * 6 + k) * ROWS + (b + 1) * COLS]
                     for h in range(2)
@@ -114,8 +124,10 @@
                 ],
                 axis=1,
             )
-            out_ref[b, k * rows : (k + 1) * rows, :] = block
-            out_ref[2 + b, k * rows : (k + 1) * rows, :] = block
+            for b in range(2)
+        ]
+        keep_ref[k * rows : (k + 1) * rows, :] = jnp.where(core == 0, blocks[0], blocks[1])
+        send_ref[k * rows : (k + 1) * rows, :] = jnp.where(core == 0, blocks[1], blocks[0])
 
 
 def left_kernel(x_ref, out_ref):
@@ -127,39 +139,45 @@
         )
 
 
-def contract_kernel(own_ref, other_ref, right_ref, core_ref, send_ref, total):
-    core = core_ref[0]
-    own, other = own_ref[...], other_ref[...]
-    left = [jnp.where(core == b, own, other) for b in range(2)]
-    for side in range(2):
+def product_kernel(left_ref, here_ref, mirror_ref, side_ref, total_ref):
+    left = left_ref[...]
+    for side, ref in ((side_ref[0], here_ref), (1 - side_ref[0], mirror_ref)):
+        right = ref[...]
         part = jnp.zeros((JSPAN, SIDE), F32)
-        for b in range(2):
-            right = right_ref[side * 2 + b]
-            for h in range(2):
-                part += dot(right[:, h * JSPAN : (h + 1) * JSPAN], left[b][h * JSPAN : (h + 1) * JSPAN], ((0,), (0,)))
+        for h in range(2):
+            part += dot(right[:, h * JSPAN : (h + 1) * JSPAN], left[h * JSPAN : (h + 1) * JSPAN], ((0,), (0,)))
         for rp in range(RPOS):
-            row = (rp // 2) * 4 + x_of(side, rp % 2)
+            x = jnp.where(side == 0, rp % 2, 3 - rp % 2)
+            rows = pl.ds(pl.multiple_of(((rp // 2) * 4 + x) * COLS, 8), COLS)
             for t in range(SIDE // LANES):
-                total[t, row * COLS : (row + 1) * COLS, :] = part[rp * COLS : (rp + 1) * COLS, t * LANES : (t + 1) * LANES]
+                total_ref[t, rows, :] = part[rp * COLS : (rp + 1) * COLS, t * LANES : (t + 1) * LANES]
+
+
+def pack_kernel(here_ref, core_ref, send_ref, total):
+    total[...] = here_ref[...] + core_ref[...]
     rows = 2 * QPOS
     blocks = [
         jnp.concatenate([total[t, pl.ds(j, rows, stride=HALF), :] for t in range(SIDE // LANES)], axis=1)
         for j in range(HALF)
     ]
+    base = (functools.reduce(jnp.add, blocks) * (1.0 / HALF)).astype(BF16).astype(F32)
+    blocks = [block - base for block in blocks] + [base]
     for rp in range(RPOS):
         piece = jnp.concatenate([block[:, rp * ROWS : (rp + 1) * ROWS] for block in blocks], axis=1)
-        send_ref[rp * QPOS : (rp + 1) * QPOS] = piece.astype(BF16).reshape(QPOS, 2, SPAN)
+        send_ref[rp * QPOS : (rp + 1) * QPOS] = piece.astype(BF16).reshape(QPOS, 2, SPAN + ROWS)
 
 
 def update_kernel(x_ref, gate_ref, gain_ref, bias_ref, w_ref, out_ref, pairs, tokens):
-    arrived = x_ref[...].reshape(2 * WIDTH, SPAN).astype(F32)
-    tiles = pl.cdiv(SPAN, LANES)
+    arrived = x_ref[...].reshape(2 * WIDTH, SPAN + ROWS).astype(F32)
+    tiles = pl.cdiv(SPAN + ROWS, LANES)
     for t in range(tiles):
         tile = arrived[:, t * LANES : (t + 1) * LANES]
         pairs[t, :, : tile.shape[1]] = tile
     for half in range(2):
         values = [pairs[t, pl.ds(half, WIDTH, stride=2), :] for t in range(tiles)]
-        values = jnp.concatenate(values, axis=1)[:, :SPAN]
+        values = jnp.concatenate(values, axis=1)
+        base = values[:, SPAN : SPAN + ROWS]
+        values = values[:, :SPAN] + jnp.concatenate([base] * HALF, axis=1)
         mean = jnp.mean(values, axis=0, keepdims=True)
         centred = values - mean
         var = jnp.mean(centred * centred, axis=0, keepdims=True)
@@ -175,35 +193,64 @@
 ):
     shape = jax.ShapeDtypeStruct
     count = ROWS * COLS
-    send, normed = call(
+    given = pair.reshape(count, WIDTH), pair_mask.T, in_gain[None], in_bias[None], proj_weight
+    send, normed = pl.pallas_call(
         factors_kernel,
-        (shape((WIDTH, 2, 2 * SPAN), BF16), shape((count, WIDTH), BF16)),
-        (pltpu.VMEM((count, WIDTH), F32), pltpu.VMEM((2 * SPAN // LANES, 2 * WIDTH, LANES), F32)),
-        "factors",
-    )(pair.reshape(count, WIDTH), pair_mask.T, in_gain[None], in_bias[None], proj_weight)
+        out_shape=(shape((WIDTH, 2, 2 * SPAN), BF16), shape((count, WIDTH), BF16)),
+        in_specs=[pl.BlockSpec(memory_space=pl.ANY)] * 5,
+        scratch_shapes=[pltpu.VMEM(value.shape, value.dtype) for value in given]
+        + [
+            pltpu.VMEM((count, WIDTH), F32),
+            pltpu.VMEM((2 * SPAN // LANES, 2 * WIDTH, LANES), F32),
+            pltpu.SemaphoreType.DMA((5,)),
+        ],
+        compiler_params=pltpu.CompilerParams(vmem_limit_bytes=56 * 2**20),
+        name="factors",
+    )(*given)
     exchange = functools.partial(
         lax.all_to_all, axis_name=AXES, split_axis=0, concat_axis=0, axis_index_groups=channel_groups(), tiled=True
     )
+    core = lax.rem(lax.axis_index("col"), 2).astype(jnp.int32).reshape(1)
+    side = (lax.rem(lax.axis_index("row"), 4) // 2).astype(jnp.int32).reshape(1)
+    vmem, smem = pl.BlockSpec(memory_space=pltpu.VMEM), pl.BlockSpec(memory_space=pltpu.SMEM)
     both = exchange(send)
     gate = call(gate_kernel, shape((count, WIDTH), F32), name="gate")(normed, gate_weight)
-    right = call(right_kernel, shape((4, JSPAN, SIDE), BF16), name="right")(both)
-    right = lax.all_to_all(right, AXES, 0, 0, axis_index_groups=quad_groups(), tiled=True)
+    keep, away = pl.pallas_call(
+        right_kernel,
+        out_shape=(shape((JSPAN, SIDE), BF16),) * 2,
+        in_specs=[vmem, smem],
+        compiler_params=pltpu.CompilerParams(vmem_limit_bytes=16 * 2**20),
+        name="right",
+    )(both, core)
+    away_mirror = lax.ppermute(away, AXES, swap(True, False))
+    keep_mirror = lax.ppermute(keep, AXES, swap(True, False))
     left = call(left_kernel, shape((SIDE, SIDE), BF16), name="left")(both)
-    other = lax.ppermute(left, AXES, core_swap())
-    core = lax.rem(lax.axis_index("col"), 2).astype(jnp.int32).reshape(1)
-    combined = pl.pallas_call(
-        contract_kernel,
-        out_shape=shape((RPOS * QPOS, 2, SPAN), BF16),
-        in_specs=[pl.BlockSpec(memory_space=pltpu.VMEM)] * 3 + [pl.BlockSpec(memory_space=pltpu.SMEM)],
-        scratch_shapes=[pltpu.VMEM((SIDE // LANES, SIDE, LANES), F32)],
+    product = functools.partial(
+        pl.pallas_call,
+        product_kernel,
+        out_shape=shape((SIDE // LANES, SIDE, LANES), F32),
+        in_specs=[vmem] * 3 + [smem],
         compiler_params=pltpu.CompilerParams(vmem_limit_bytes=16 * 2**20),
-        name="contract",
-    )(left, other, right, core)
+    )
+    size = SIDE * SIDE * SIDE * 2
+    partial = product(name="away", cost_estimate=pl.CostEstimate(flops=size, bytes_accessed=0, transcendentals=0))(
+        left, away, away_mirror, side
+    )
+    partial = lax.ppermute(partial, AXES, swap(False, True))
+    total = product(name="keep", cost_estimate=pl.CostEstimate(flops=size * WEIGHT, bytes_accessed=0, transcendentals=0))(
+        left, keep, keep_mirror, side
+    )
+    combined = call(
+        pack_kernel,
+        shape((RPOS * QPOS, 2, SPAN + ROWS), BF16),
+        (pltpu.VMEM((SIDE // LANES, SIDE, LANES), F32),),
+        "pack",
+    )(total, partial)
     combined = exchange(combined)
     update = call(
         update_kernel,
         shape((count, WIDTH), BF16),
-        (pltpu.VMEM((pl.cdiv(SPAN, LANES), 2 * WIDTH, LANES), F32), pltpu.VMEM((count, WIDTH), F32)),
+        (pltpu.VMEM((pl.cdiv(SPAN + ROWS, LANES), 2 * WIDTH, LANES), F32), pltpu.VMEM((count, WIDTH), F32)),
         "update",
     )(combined, gate, out_gain[:, None], out_bias[:, None], out_weight)
     return update.reshape(ROWS, COLS, WIDTH)

time: 84.8 us -> 82.7 us (0.975)
  blocking collectives: 38.3 us -> 0 us
  starting transfers between devices: 14.3 us -> 38.9 us
  waiting for transfers between devices: 19 us -> 32.5 us
  local copies, waits for them, and re-layouts: 5.42 us -> 2.18 us
  Pallas kernels: 6.4 us -> 7.95 us
    all_to_all x1 -> x0, blocking collectives: 38.3 us -> none  [per_device(): both = exchange(send)]
    all_to_all x1, starting transfers between devices: 6.05 us -> 19.3 us  [per_device(): both = exchange(send)]
    all_to_all x1, waiting for transfers between devices: 6.1 us -> 19.2 us  [per_device(): both = exchange(send)]
    ppermute x1 -> x3, starting transfers between devices: 1.95 us -> 13.1 us  [the longest x1 6.62 us: per_device(): partial = lax.ppermute(partial, AXES, swap(False, True))]
    unnamed x18 -> x10, local copies, waits for them, and re-layouts: 5.19 us -> 1.95 us
    pallas_call x3 -> x5, Pallas kernels: 4.45 us -> 5.93 us  [the longest x1 3.23 us: per_device(): pl.pallas_call(factors_kernel, out_shape=(shape((WIDTH, 2, 2 * SPAN), BF1...]
  transfers between devices with their start and end apart: 3 -> 5, of which waited for: 3 -> 4; matrix products, arithmetic and copies ran while one was open for 0% -> 0% of each run, Pallas kernels for 1% -> 2%
where the time goes in v2:
time: 82.7 us; the launch traced here: 81.6 us
  starting transfers between devices  38.9 us (47%)
  waiting for transfers between devices  32.5 us (39%)
  Pallas kernels  7.95 us (10%)
  local copies, waits for them, and re-layouts  2.18 us (3%)
    all_to_all x1, starting transfers between devices, per_device(): both = exchange(send)  19.3 us
    all_to_all x1, waiting for transfers between devices, per_device(): both = exchange(send)  19.2 us
    all_to_all x1, waiting for transfers between devices, per_device(): combined = exchange(combined)  11.9 us
    ppermute x1, starting transfers between devices, per_device(): partial = lax.ppermute(partial, AXES, swap(False, True))  6.62 us
    all_to_all x1, starting transfers between devices, per_device(): combined = exchange(combined)  6.43 us
    ppermute x1, starting transfers between devices, per_device(): away_mirror = lax.ppermute(away, AXES, swap(True, False))  3.72 us
    pallas_call x1, Pallas kernels, per_device(): pl.pallas_call(factors_kernel, out_shape=(shape((WIDTH, 2, 2 * SPAN), BF1...  3.23 us
    ppermute x1, starting transfers between devices, per_device(): keep_mirror = lax.ppermute(keep, AXES, swap(True, False))  2.77 us
  transfers between devices with their start and end apart: 5, of which 4 were waited for; matrix products, arithmetic and copies ran while one was open for 0% of the time, Pallas kernels for 2%

profile of v2, /device:TPU:1, one launch (start us, length us, event | category | flops | bytes accessed | tf_op | source)
XLA Modules:
  0.0 81.6 jit_solution(4152528254858983031)
XLA Ops:
  0.0 3.2 %factors.1 = (bf16[128,2,1152]{2,1,0:T(2,128)(2,1)}, bf16[1152,128]{1,0:T(8,128)(2,1)}) custom-call(bf16[1152,128]{1,0:T(8,128)(2,1)} %bitcast.9, s32[24,48]{1,0:T(8,128)} %bitcast.10, f32[1,128]{1,0:T(1,128)} %bitcast.11, f32[1,128]{1,0:T(1,128)} %bitcast.12, bf16[128,512]{1,0:T(8,128)(2,1)} %refs_4_.1), custom_call_target="tpu_custom_call" | custom-call | tf_op jit(solution)/shard_map/factors/pallas_call | solution.py:197
  3.2 19.3 %all-to-all-start = ((bf16[128,2,1152]{2,1,0:T(2,128)(2,1)}), bf16[128,2,1152]{2,1,0:T(2,128)(2,1)S(1)}, u32[]{:S(2)}, u32[]{:S(2)}) async-start(bf16[128,2,1152]{2,1,0:T(2,128)(2,1)} %get-tuple-element.9), calls=%async_computation | async-start | bytes 1179648 | tf_op jit(solution)/shard_map/all_to_all | solution.py:216
  22.5 19.2 %all-to-all-done.x_ref = bf16[128,2,1152]{2,1,0:T(2,128)(2,1)S(1)} async-done(((bf16[128,2,1152]{2,1,0:T(2,128)(2,1)}), bf16[128,2,1152]{2,1,0:T(2,128)(2,1)S(1)}, u32[]{:S(2)}, u32[]{:S(2)}) %all-to-all-start) | async-done | bytes 589856 | tf_op jit(solution)/shard_map/all_to_all | solution.py:216
  41.8 0.5 right.1
  42.3 3.7 %collective-permute-start.1 = (bf16[192,384]{1,0:T(8,128)(2,1)S(1)}, bf16[192,384]{1,0:T(8,128)(2,1)S(1)}, u32[]{:S(2)}, u32[]{:S(2)}) collective-permute-start(bf16[192,384]{1,0:T(8,128)(2,1)S(1)} %get-tuple-element.11.here_ref), channel_id=1, source_target_pairs={{0,96},{1,97},{2,98},{3,99},{4,100},{5,101},{6,102},{7,103},{8,104... | collective-permute-start | bytes 442376 | tf_op jit(solution)/shard_map/ppermute | solution.py:225
  46.0 2.8 %collective-permute-start = (bf16[192,384]{1,0:T(8,128)(2,1)S(1)}, bf16[192,384]{1,0:T(8,128)(2,1)S(1)}, u32[]{:S(2)}, u32[]{:S(2)}) collective-permute-start(bf16[192,384]{1,0:T(8,128)(2,1)S(1)} %get-tuple-element.10.here_ref), channel_id=1, source_target_pairs={{0,96},{1,97},{2,98},{3,99},{4,100},{5,101},{6,102},{7,103},{8,104... | collective-permute-start | bytes 442376 | tf_op jit(solution)/shard_map/ppermute | solution.py:226
  48.8 0.3 left.1.left_ref
  49.2 0.3 collective-permute-done.1.mirror_ref
  49.4 0.5 away.1
  50.0 6.6 %collective-permute-start.2 = (f32[3,384,128]{2,1,0:T(8,128)S(1)}, f32[3,384,128]{2,1,0:T(8,128)S(1)}, u32[]{:S(2)}, u32[]{:S(2)}) collective-permute-start(f32[3,384,128]{2,1,0:T(8,128)S(1)} %away.1), channel_id=1, source_target_pairs={{0,1},{1,0},{2,3},{3,2},{4,5},{5,4},{6,7},{7,6},{8,9},{9,8},{10,11... | collective-permute-start | bytes 1769480 | tf_op jit(solution)/shard_map/ppermute | solution.py:239
  56.6 0.0 collective-permute-done.mirror_ref
  56.6 0.5 keep.1.here_ref
  57.1 1.0 %collective-permute-done.2.core_ref = f32[3,384,128]{2,1,0:T(8,128)S(1)} collective-permute-done((f32[3,384,128]{2,1,0:T(8,128)S(1)}, f32[3,384,128]{2,1,0:T(8,128)S(1)}, u32[]{:S(2)}, u32[]{:S(2)}) %collective-permute-start.2) | collective-permute-done | bytes 589856 | tf_op jit(solution)/shard_map/ppermute | solution.py:239
  58.2 1.1 %pack.1 = bf16[128,2,624]{2,1,0:T(2,128)(2,1)} custom-call(f32[3,384,128]{2,1,0:T(8,128)S(1)} %keep.1.here_ref, f32[3,384,128]{2,1,0:T(8,128)S(1)} %collective-permute-done.2.core_ref), custom_call_target="tpu_custom_call" | custom-call | tf_op jit(solution)/shard_map/pack/pallas_call | solution.py:243
  59.3 0.0 copy-start
  59.3 6.4 %all-to-all-start.1 = ((bf16[128,2,624]{2,1,0:T(2,128)(2,1)}), bf16[128,2,624]{2,1,0:T(2,128)(2,1)S(1)}, u32[]{:S(2)}, u32[]{:S(2)}) async-start(bf16[128,2,624]{2,1,0:T(2,128)(2,1)} %pack.1), calls=%async_computation.1 | async-start | bytes 655360 | tf_op jit(solution)/shard_map/all_to_all | solution.py:249
  65.7 0.0 copy-start.3
  65.8 0.6 copy-done.3
  66.4 0.1 copy.10.gain_ref
  66.5 0.0 copy-start.4
  66.5 0.7 copy-done.4
  67.2 0.0 copy-start.1
  67.2 0.1 copy.11.bias_ref
  67.3 0.0 copy-done
  67.3 0.6 copy-done.1
  67.9 0.0 copy-start.2
  67.9 0.2 gate.1.gate_ref
  68.2 11.9 %all-to-all-done.1.x_ref = bf16[128,2,624]{2,1,0:T(2,128)(2,1)S(1)} async-done(((bf16[128,2,624]{2,1,0:T(2,128)(2,1)}), bf16[128,2,624]{2,1,0:T(2,128)(2,1)S(1)}, u32[]{:S(2)}, u32[]{:S(2)}) %all-to-all-start.1) | async-done | bytes 319520 | tf_op jit(solution)/shard_map/all_to_all | solution.py:249
  80.1 0.0 copy-done.2
  80.1 1.5 %update.1 = bf16[1152,128]{1,0:T(8,128)(2,1)} custom-call(bf16[128,2,624]{2,1,0:T(2,128)(2,1)S(1)} %all-to-all-done.1.x_ref, f32[1152,128]{1,0:T(8,128)S(1)} %gate.1.gate_ref, f32[128,1]{1,0:T(8,128)S(1)} %copy.10.gain_ref, f32[128,1]{1,0:T(8,128)S(1)} %copy.11.bias_ref, bf16[128,128]{1,0:T(8,128)(2,1)S(1)} %copy-done.2), custom_call_target="tpu_custom_call" | custom-call | tf_op jit(solution)/shard_map/update/pallas_call | solution.py:250
Async XLA Ops:
  3.2 38.6 %all-to-all-start = ((bf16[128,2,1152]{2,1,0:T(2,128)(2,1)}), bf16[128,2,1152]{2,1,0:T(2,128)(2,1)S(1)}, u32[]{:S(2)}, u32[]{:S(2)}) async-start(bf16[128,2,1152]{2,1,0:T(2,128)(2,1)} %get-tuple-element.9), calls=%async_computation | async-start | bytes 1179648 | tf_op jit(solution)/shard_map/all_to_all | solution.py:216
  42.3 7.1 %collective-permute-start.1 = (bf16[192,384]{1,0:T(8,128)(2,1)S(1)}, bf16[192,384]{1,0:T(8,128)(2,1)S(1)}, u32[]{:S(2)}, u32[]{:S(2)}) collective-permute-start(bf16[192,384]{1,0:T(8,128)(2,1)S(1)} %get-tuple-element.11.here_ref), channel_id=1, source_target_pairs={{0,96},{1,97},{2,98},{3,99},{4,100},{5,101},{6,102},{7,103},{8,104... | collective-permute-start | bytes 442376 | tf_op jit(solution)/shard_map/ppermute | solution.py:225
  46.0 10.5 %collective-permute-start = (bf16[192,384]{1,0:T(8,128)(2,1)S(1)}, bf16[192,384]{1,0:T(8,128)(2,1)S(1)}, u32[]{:S(2)}, u32[]{:S(2)}) collective-permute-start(bf16[192,384]{1,0:T(8,128)(2,1)S(1)} %get-tuple-element.10.here_ref), channel_id=1, source_target_pairs={{0,96},{1,97},{2,98},{3,99},{4,100},{5,101},{6,102},{7,103},{8,104... | collective-permute-start | bytes 442376 | tf_op jit(solution)/shard_map/ppermute | solution.py:226
  50.0 8.2 %collective-permute-start.2 = (f32[3,384,128]{2,1,0:T(8,128)S(1)}, f32[3,384,128]{2,1,0:T(8,128)S(1)}, u32[]{:S(2)}, u32[]{:S(2)}) collective-permute-start(f32[3,384,128]{2,1,0:T(8,128)S(1)} %away.1), channel_id=1, source_target_pairs={{0,1},{1,0},{2,3},{3,2},{4,5},{5,4},{6,7},{7,6},{8,9},{9,8},{10,11... | collective-permute-start | bytes 1769480 | tf_op jit(solution)/shard_map/ppermute | solution.py:239
  59.3 8.0 %copy-start = (bf16[1152,128]{1,0:T(8,128)(2,1)S(1)}, bf16[1152,128]{1,0:T(8,128)(2,1)}, u32[]{:S(2)}) copy-start(bf16[1152,128]{1,0:T(8,128)(2,1)} %get-tuple-element.12.normed_ref) | copy-start | bytes 884740
  59.3 20.8 %all-to-all-start.1 = ((bf16[128,2,624]{2,1,0:T(2,128)(2,1)}), bf16[128,2,624]{2,1,0:T(2,128)(2,1)S(1)}, u32[]{:S(2)}, u32[]{:S(2)}) async-start(bf16[128,2,624]{2,1,0:T(2,128)(2,1)} %pack.1), calls=%async_computation.1 | async-start | bytes 655360 | tf_op jit(solution)/shard_map/all_to_all | solution.py:249
  65.7 0.7 copy-start.3
  66.5 0.7 copy-start.4
  67.2 0.8 copy-start.1
  67.9 12.2 %copy-start.2 = (bf16[128,128]{1,0:T(8,128)(2,1)S(1)}, bf16[128,128]{1,0:T(8,128)(2,1)}, u32[]{:S(2)}) copy-start(bf16[128,128]{1,0:T(8,128)(2,1)} %w_ref.3) | copy-start | bytes 98308

commit v3 on v2

--- a/solution.py
+++ b/solution.py
@@ -11,7 +11,7 @@
 F32 = jnp.float32
 AXES = ("row", "col")
 ROWS, COLS, WIDTH = 48, 24, 128
-WEIGHT = 100
+COST_SCALE = 100
 HALF = COLS // 2
 SPAN = HALF * ROWS
 RPOS, QPOS = 8, 16
@@ -130,31 +130,35 @@
         send_ref[k * rows : (k + 1) * rows, :] = jnp.where(core == 0, blocks[1], blocks[0])
 
 
-def left_kernel(x_ref, out_ref):
+def left_kernel(x_ref, away_ref, out_ref):
     x = x_ref[...].reshape(RPOS * QPOS * 2, 2 * SPAN)[:, :SPAN]
     rows = 2 * QPOS
     for k in range(HALF):
         out_ref[k * rows : (k + 1) * rows, :] = jnp.concatenate(
             [x[rp * rows : (rp + 1) * rows, k * ROWS : (k + 1) * ROWS] for rp in range(RPOS)], axis=1
         )
-
-
-def product_kernel(left_ref, here_ref, mirror_ref, side_ref, total_ref):
-    left = left_ref[...]
-    for side, ref in ((side_ref[0], here_ref), (1 - side_ref[0], mirror_ref)):
-        right = ref[...]
+    out_ref[SIDE:, :] = away_ref[...]
+
+
+def add_products(left, here, mirror, side, total, earlier=None):
+    for at, right in ((side, here), (1 - side, mirror)):
         part = jnp.zeros((JSPAN, SIDE), F32)
         for h in range(2):
             part += dot(right[:, h * JSPAN : (h + 1) * JSPAN], left[h * JSPAN : (h + 1) * JSPAN], ((0,), (0,)))
         for rp in range(RPOS):
-            x = jnp.where(side == 0, rp % 2, 3 - rp % 2)
+            x = jnp.where(at == 0, rp % 2, 3 - rp % 2)
             rows = pl.ds(pl.multiple_of(((rp // 2) * 4 + x) * COLS, 8), COLS)
             for t in range(SIDE // LANES):
-                total_ref[t, rows, :] = part[rp * COLS : (rp + 1) * COLS, t * LANES : (t + 1) * LANES]
-
-
-def pack_kernel(here_ref, core_ref, send_ref, total):
-    total[...] = here_ref[...] + core_ref[...]
+                piece = part[rp * COLS : (rp + 1) * COLS, t * LANES : (t + 1) * LANES]
+                total[t, rows, :] = piece if earlier is None else piece + earlier[t, rows, :]
+
+
+def own_kernel(bundle_ref, keep_ref, mirror_ref, side_ref, total_ref):
+    add_products(bundle_ref[:SIDE], keep_ref[...], mirror_ref[...], side_ref[0], total_ref)
+
+
+def contract_kernel(bundle_ref, cross_ref, own_ref, side_ref, send_ref, total):
+    add_products(bundle_ref[:SIDE], bundle_ref[SIDE:], cross_ref[...], side_ref[0], total, own_ref)
     rows = 2 * QPOS
     blocks = [
         jnp.concatenate([total[t, pl.ds(j, rows, stride=HALF), :] for t in range(SIDE // LANES)], axis=1)
@@ -222,30 +226,26 @@
         compiler_params=pltpu.CompilerParams(vmem_limit_bytes=16 * 2**20),
         name="right",
     )(both, core)
-    away_mirror = lax.ppermute(away, AXES, swap(True, False))
-    keep_mirror = lax.ppermute(keep, AXES, swap(True, False))
-    left = call(left_kernel, shape((SIDE, SIDE), BF16), name="left")(both)
-    product = functools.partial(
-        pl.pallas_call,
-        product_kernel,
+    mirror = lax.ppermute(keep, AXES, swap(True, False))
+    cross = lax.ppermute(away, AXES, swap(True, True))
+    bundle = call(left_kernel, shape((SIDE + JSPAN, SIDE), BF16), name="left")(both, away)
+    bundle_core = lax.ppermute(bundle, AXES, swap(False, True))
+    own = pl.pallas_call(
+        own_kernel,
         out_shape=shape((SIDE // LANES, SIDE, LANES), F32),
         in_specs=[vmem] * 3 + [smem],
         compiler_params=pltpu.CompilerParams(vmem_limit_bytes=16 * 2**20),
-    )
-    size = SIDE * SIDE * SIDE * 2
-    partial = product(name="away", cost_estimate=pl.CostEstimate(flops=size, bytes_accessed=0, transcendentals=0))(
-        left, away, away_mirror, side
-    )
-    partial = lax.ppermute(partial, AXES, swap(False, True))
-    total = product(name="keep", cost_estimate=pl.CostEstimate(flops=size * WEIGHT, bytes_accessed=0, transcendentals=0))(
-        left, keep, keep_mirror, side
-    )
-    combined = call(
-        pack_kernel,
-        shape((RPOS * QPOS, 2, SPAN + ROWS), BF16),
-        (pltpu.VMEM((SIDE // LANES, SIDE, LANES), F32),),
-        "pack",
-    )(total, partial)
+        cost_estimate=pl.CostEstimate(flops=SIDE * SIDE * SIDE * 2 * COST_SCALE, bytes_accessed=0, transcendentals=0),
+        name="own",
+    )(bundle, keep, mirror, side)
+    combined = pl.pallas_call(
+        contract_kernel,
+        out_shape=shape((RPOS * QPOS, 2, SPAN + ROWS), BF16),
+        in_specs=[vmem] * 3 + [smem],
+        scratch_shapes=[pltpu.VMEM((SIDE // LANES, SIDE, LANES), F32)],
+        compiler_params=pltpu.CompilerParams(vmem_limit_bytes=16 * 2**20),
+        name="contract",
+    )(bundle_core, cross, own, side)
     combined = exchange(combined)
     update = call(
         update_kernel,

time: 82.7 us -> 81.4 us (0.984)
    ppermute x3, starting transfers between devices: 13.1 us -> 11.2 us  [the longest x1 5.54 us: per_device(): cross = lax.ppermute(away, AXES, swap(True, True))]
    all_to_all x1, starting transfers between devices: 6.43 us -> 7.66 us  [per_device(): combined = exchange(combined)]
    pallas_call x4 -> x3, Pallas kernels: 2.49 us -> 2.42 us  [the longest x1 1.57 us: per_device(): pl.pallas_call(contract_kernel, out_shape=shape((RPOS * QPOS, 2, SPAN + R...]
  transfers between devices with their start and end apart: 5 -> 5, of which waited for: 4 -> 4; matrix products, arithmetic and copies ran while one was open for 0% -> 0% of each run, Pallas kernels for 2% -> 1%
where the time goes in v3:
time: 81.4 us; the launch traced here: 80.2 us
  starting transfers between devices  38.1 us (47%)
  waiting for transfers between devices  31.9 us (39%)
  Pallas kernels  7.88 us (10%)
  local copies, waits for them, and re-layouts  2.18 us (3%)
    all_to_all x1, starting transfers between devices, per_device(): both = exchange(send)  19.3 us
    all_to_all x1, waiting for transfers between devices, per_device(): both = exchange(send)  19.2 us
    all_to_all x1, waiting for transfers between devices, per_device(): combined = exchange(combined)  11.4 us
    all_to_all x1, starting transfers between devices, per_device(): combined = exchange(combined)  7.66 us
    ppermute x1, starting transfers between devices, per_device(): cross = lax.ppermute(away, AXES, swap(True, True))  5.54 us
    ppermute x1, starting transfers between devices, per_device(): mirror = lax.ppermute(keep, AXES, swap(True, False))  3.72 us
    pallas_call x1, Pallas kernels, per_device(): pl.pallas_call(factors_kernel, out_shape=(shape((WIDTH, 2, 2 * SPAN), BF1...  3.23 us
    unnamed x10, local copies, waits for them, and re-layouts  1.95 us
  transfers between devices with their start and end apart: 5, of which 4 were waited for; matrix products, arithmetic and copies ran while one was open for 0% of the time, Pallas kernels for 1%

profile of v3, /device:TPU:1, one launch (start us, length us, event | category | flops | bytes accessed | tf_op | source)
XLA Modules:
  0.0 80.2 jit_solution(9655432039715312503)
XLA Ops:
  0.0 3.2 %factors.1 = (bf16[128,2,1152]{2,1,0:T(2,128)(2,1)}, bf16[1152,128]{1,0:T(8,128)(2,1)}) custom-call(bf16[1152,128]{1,0:T(8,128)(2,1)} %bitcast.9, s32[24,48]{1,0:T(8,128)} %bitcast.10, f32[1,128]{1,0:T(1,128)} %bitcast.11, f32[1,128]{1,0:T(1,128)} %bitcast.12, bf16[128,512]{1,0:T(8,128)(2,1)} %refs_4_.1), custom_call_target="tpu_custom_call" | custom-call | tf_op jit(solution)/shard_map/factors/pallas_call | solution.py:201
  3.2 19.3 %all-to-all-start = ((bf16[128,2,1152]{2,1,0:T(2,128)(2,1)}), bf16[128,2,1152]{2,1,0:T(2,128)(2,1)S(1)}, u32[]{:S(2)}, u32[]{:S(2)}) async-start(bf16[128,2,1152]{2,1,0:T(2,128)(2,1)} %get-tuple-element.9), calls=%async_computation | async-start | bytes 1179648 | tf_op jit(solution)/shard_map/all_to_all | solution.py:220
  22.5 19.2 %all-to-all-done.x_ref = bf16[128,2,1152]{2,1,0:T(2,128)(2,1)S(1)} async-done(((bf16[128,2,1152]{2,1,0:T(2,128)(2,1)}), bf16[128,2,1152]{2,1,0:T(2,128)(2,1)S(1)}, u32[]{:S(2)}, u32[]{:S(2)}) %all-to-all-start) | async-done | bytes 589856 | tf_op jit(solution)/shard_map/all_to_all | solution.py:220
  41.8 0.5 right.1
  42.3 3.7 %collective-permute-start.2 = (bf16[192,384]{1,0:T(8,128)(2,1)S(1)}, bf16[192,384]{1,0:T(8,128)(2,1)S(1)}, u32[]{:S(2)}, u32[]{:S(2)}) collective-permute-start(bf16[192,384]{1,0:T(8,128)(2,1)S(1)} %get-tuple-element.11.keep_ref), channel_id=1, source_target_pairs={{0,96},{1,97},{2,98},{3,99},{4,100},{5,101},{6,102},{7,103},{8,104... | collective-permute-start | bytes 442376 | tf_op jit(solution)/shard_map/ppermute | solution.py:229
  46.1 5.5 %collective-permute-start.1 = (bf16[192,384]{1,0:T(8,128)(2,1)S(1)}, bf16[192,384]{1,0:T(8,128)(2,1)S(1)}, u32[]{:S(2)}, u32[]{:S(2)}) collective-permute-start(bf16[192,384]{1,0:T(8,128)(2,1)S(1)} %get-tuple-element.10.away_ref), channel_id=1, source_target_pairs={{0,97},{1,96},{2,99},{3,98},{4,101},{5,100},{6,103},{7,102},{8,105... | collective-permute-start | bytes 442376 | tf_op jit(solution)/shard_map/ppermute | solution.py:230
  51.6 0.3 left.1.bundle_ref
  51.9 1.9 %collective-permute-start = (bf16[576,384]{1,0:T(8,128)(2,1)S(1)}, bf16[576,384]{1,0:T(8,128)(2,1)S(1)}, u32[]{:S(2)}, u32[]{:S(2)}) collective-permute-start(bf16[576,384]{1,0:T(8,128)(2,1)S(1)} %left.1.bundle_ref), channel_id=1, source_target_pairs={{0,1},{1,0},{2,3},{3,2},{4,5},{5,4},{6,7},{7,6},{8,9},{9,8},{10,11... | collective-permute-start | bytes 1327112 | tf_op jit(solution)/shard_map/ppermute | solution.py:232
  53.9 0.0 collective-permute-done.2.mirror_ref
  53.9 0.5 own.1.own_ref
  54.4 0.3 collective-permute-done.1.cross_ref
  54.7 0.9 %collective-permute-done.bundle_ref = bf16[576,384]{1,0:T(8,128)(2,1)S(1)} collective-permute-done((bf16[576,384]{1,0:T(8,128)(2,1)S(1)}, bf16[576,384]{1,0:T(8,128)(2,1)S(1)}, u32[]{:S(2)}, u32[]{:S(2)}) %collective-permute-start) | collective-permute-done | bytes 442400 | tf_op jit(solution)/shard_map/ppermute | solution.py:232
  55.6 1.6 %contract.1 = bf16[128,2,624]{2,1,0:T(2,128)(2,1)} custom-call(bf16[576,384]{1,0:T(8,128)(2,1)S(1)} %collective-permute-done.bundle_ref, bf16[192,384]{1,0:T(8,128)(2,1)S(1)} %collective-permute-done.1.cross_ref, f32[3,384,128]{2,1,0:T(8,128)S(1)} %own.1.own_ref, s32[1]{0:T(128)} %bitcast.5.side_ref), custom_call_target="tpu_custom_call" | custom-call | tf_op jit(solution)/shard_map/contract/pallas_call | solution.py:241
  57.2 0.0 copy-start
  57.2 7.7 %all-to-all-start.1 = ((bf16[128,2,624]{2,1,0:T(2,128)(2,1)}), bf16[128,2,624]{2,1,0:T(2,128)(2,1)S(1)}, u32[]{:S(2)}, u32[]{:S(2)}) async-start(bf16[128,2,624]{2,1,0:T(2,128)(2,1)} %contract.1), calls=%async_computation.1 | async-start | bytes 655360 | tf_op jit(solution)/shard_map/all_to_all | solution.py:249
  64.9 0.0 copy-start.3
  64.9 0.6 copy-done.3
  65.5 0.1 copy.10.gain_ref
  65.6 0.0 copy-start.4
  65.6 0.7 copy-done.4
  66.3 0.0 copy-start.1
  66.3 0.1 copy.11.bias_ref
  66.4 0.0 copy-done
  66.4 0.6 copy-done.1
  67.0 0.0 copy-start.2
  67.0 0.2 gate.1.gate_ref
  67.3 11.4 %all-to-all-done.1.x_ref = bf16[128,2,624]{2,1,0:T(2,128)(2,1)S(1)} async-done(((bf16[128,2,624]{2,1,0:T(2,128)(2,1)}), bf16[128,2,624]{2,1,0:T(2,128)(2,1)S(1)}, u32[]{:S(2)}, u32[]{:S(2)}) %all-to-all-start.1) | async-done | bytes 319520 | tf_op jit(solution)/shard_map/all_to_all | solution.py:249
  78.7 0.0 copy-done.2
  78.7 1.5 %update.1 = bf16[1152,128]{1,0:T(8,128)(2,1)} custom-call(bf16[128,2,624]{2,1,0:T(2,128)(2,1)S(1)} %all-to-all-done.1.x_ref, f32[1152,128]{1,0:T(8,128)S(1)} %gate.1.gate_ref, f32[128,1]{1,0:T(8,128)S(1)} %copy.10.gain_ref, f32[128,1]{1,0:T(8,128)S(1)} %copy.11.bias_ref, bf16[128,128]{1,0:T(8,128)(2,1)S(1)} %copy-done.2), custom_call_target="tpu_custom_call" | custom-call | tf_op jit(solution)/shard_map/update/pallas_call | solution.py:250
Async XLA Ops:
  3.2 38.6 %all-to-all-start = ((bf16[128,2,1152]{2,1,0:T(2,128)(2,1)}), bf16[128,2,1152]{2,1,0:T(2,128)(2,1)S(1)}, u32[]{:S(2)}, u32[]{:S(2)}) async-start(bf16[128,2,1152]{2,1,0:T(2,128)(2,1)} %get-tuple-element.9), calls=%async_computation | async-start | bytes 1179648 | tf_op jit(solution)/shard_map/all_to_all | solution.py:220
  42.3 11.5 %collective-permute-start.2 = (bf16[192,384]{1,0:T(8,128)(2,1)S(1)}, bf16[192,384]{1,0:T(8,128)(2,1)S(1)}, u32[]{:S(2)}, u32[]{:S(2)}) collective-permute-start(bf16[192,384]{1,0:T(8,128)(2,1)S(1)} %get-tuple-element.11.keep_ref), channel_id=1, source_target_pairs={{0,96},{1,97},{2,98},{3,99},{4,100},{5,101},{6,102},{7,103},{8,104... | collective-permute-start | bytes 442376 | tf_op jit(solution)/shard_map/ppermute | solution.py:229
  46.1 8.7 %collective-permute-start.1 = (bf16[192,384]{1,0:T(8,128)(2,1)S(1)}, bf16[192,384]{1,0:T(8,128)(2,1)S(1)}, u32[]{:S(2)}, u32[]{:S(2)}) collective-permute-start(bf16[192,384]{1,0:T(8,128)(2,1)S(1)} %get-tuple-element.10.away_ref), channel_id=1, source_target_pairs={{0,97},{1,96},{2,99},{3,98},{4,101},{5,100},{6,103},{7,102},{8,105... | collective-permute-start | bytes 442376 | tf_op jit(solution)/shard_map/ppermute | solution.py:230
  51.9 3.7 %collective-permute-start = (bf16[576,384]{1,0:T(8,128)(2,1)S(1)}, bf16[576,384]{1,0:T(8,128)(2,1)S(1)}, u32[]{:S(2)}, u32[]{:S(2)}) collective-permute-start(bf16[576,384]{1,0:T(8,128)(2,1)S(1)} %left.1.bundle_ref), channel_id=1, source_target_pairs={{0,1},{1,0},{2,3},{3,2},{4,5},{5,4},{6,7},{7,6},{8,9},{9,8},{10,11... | collective-permute-start | bytes 1327112 | tf_op jit(solution)/shard_map/ppermute | solution.py:232
  57.2 9.2 %copy-start = (bf16[1152,128]{1,0:T(8,128)(2,1)S(1)}, bf16[1152,128]{1,0:T(8,128)(2,1)}, u32[]{:S(2)}) copy-start(bf16[1152,128]{1,0:T(8,128)(2,1)} %get-tuple-element.12.normed_ref) | copy-start | bytes 884740
  57.2 21.5 %all-to-all-start.1 = ((bf16[128,2,624]{2,1,0:T(2,128)(2,1)}), bf16[128,2,624]{2,1,0:T(2,128)(2,1)S(1)}, u32[]{:S(2)}, u32[]{:S(2)}) async-start(bf16[128,2,624]{2,1,0:T(2,128)(2,1)} %contract.1), calls=%async_computation.1 | async-start | bytes 655360 | tf_op jit(solution)/shard_map/all_to_all | solution.py:249
  64.9 0.7 copy-start.3
  65.6 0.7 copy-start.4
  66.3 0.8 copy-start.1
  67.0 11.7 %copy-start.2 = (bf16[128,128]{1,0:T(8,128)(2,1)S(1)}, bf16[128,128]{1,0:T(8,128)(2,1)}, u32[]{:S(2)}) copy-start(bf16[128,128]{1,0:T(8,128)(2,1)} %w_ref.3) | copy-start | bytes 98308

commit v4 on v3

--- a/solution.py
+++ b/solution.py
@@ -106,8 +106,11 @@
         send_ref[:, :, t * LANES : (t + 1) * LANES] = pairs[t].astype(BF16).reshape(WIDTH, 2, LANES)
 
 
-def gate_kernel(normed_ref, w_ref, gate_ref):
+def gate_kernel(normed_ref, w_ref, *rest_refs):
+    *from_refs, gate_ref, gain_ref, bias_ref, out_w_ref = rest_refs
     gate_ref[...] = sigmoid(dot(normed_ref[...], w_ref[...], ((1,), (0,))))
+    for source, target in zip(from_refs, (gain_ref, bias_ref, out_w_ref)):
+        target[...] = source[...]
 
 
 def right_kernel(x_ref, core_ref, keep_ref, send_ref):
@@ -218,7 +221,11 @@
     side = (lax.rem(lax.axis_index("row"), 4) // 2).astype(jnp.int32).reshape(1)
     vmem, smem = pl.BlockSpec(memory_space=pltpu.VMEM), pl.BlockSpec(memory_space=pltpu.SMEM)
     both = exchange(send)
-    gate = call(gate_kernel, shape((count, WIDTH), F32), name="gate")(normed, gate_weight)
+    last = out_gain[:, None], out_bias[:, None], out_weight
+    late = call(
+        gate_kernel, [shape((count, WIDTH), F32)] + [shape(value.shape, value.dtype) for value in last], name="gate"
+    )(normed, gate_weight, *last)
+    late, both = lax.optimization_barrier((late, both))
     keep, away = pl.pallas_call(
         right_kernel,
         out_shape=(shape((JSPAN, SIDE), BF16),) * 2,
@@ -252,7 +259,7 @@
         shape((count, WIDTH), BF16),
         (pltpu.VMEM((pl.cdiv(SPAN + ROWS, LANES), 2 * WIDTH, LANES), F32), pltpu.VMEM((count, WIDTH), F32)),
         "update",
-    )(combined, gate, out_gain[:, None], out_bias[:, None], out_weight)
+    )(combined, *late)
     return update.reshape(ROWS, COLS, WIDTH)
 
 

time: 81.4 us -> 80.8 us (level)
  blocking collectives: 0 us -> 21.5 us
  waiting for transfers between devices: 31.9 us -> 18 us
  starting transfers between devices: 38.1 us -> 30.6 us
    all_to_all x0 -> x1, blocking collectives: none -> 21.5 us  [per_device(): combined = exchange(combined)]
    all_to_all x1 -> x0, waiting for transfers between devices: 11.4 us -> none  [per_device(): combined = exchange(combined)]
    all_to_all x1 -> x0, starting transfers between devices: 7.66 us -> none  [per_device(): combined = exchange(combined)]
    all_to_all x1, waiting for transfers between devices: 19.2 us -> 16.8 us  [per_device(): both = exchange(send)]
  transfers between devices with their start and end apart: 5 -> 4, of which waited for: 4 -> 3; matrix products, arithmetic and copies ran while one was open for 0% -> 0% of each run, Pallas kernels for 1% -> 1%
where the time goes in v4:
time: 80.8 us; the launch traced here: 79.6 us
  starting transfers between devices  30.6 us (38%)
  blocking collectives  21.5 us (27%)
  waiting for transfers between devices  18 us (22%)
  Pallas kernels  7.18 us (9%)
  local copies, waits for them, and re-layouts  2.19 us (3%)
    all_to_all x1, blocking collectives, per_device(): combined = exchange(combined)  21.5 us
    all_to_all x1, starting transfers between devices, per_device(): both = exchange(send)  19.4 us
    all_to_all x1, waiting for transfers between devices, per_device(): both = exchange(send)  16.8 us
    ppermute x1, starting transfers between devices, per_device(): cross = lax.ppermute(away, AXES, swap(True, True))  5.54 us
    ppermute x1, starting transfers between devices, per_device(): mirror = lax.ppermute(keep, AXES, swap(True, False))  3.72 us
    pallas_call x1, Pallas kernels, per_device(): pl.pallas_call(factors_kernel, out_shape=(shape((WIDTH, 2, 2 * SPAN), BF1...  3.23 us
    unnamed x10, local copies, waits for them, and re-layouts  1.96 us
    ppermute x1, starting transfers between devices, per_device(): bundle_core = lax.ppermute(bundle, AXES, swap(False, True))  1.92 us
  transfers between devices with their start and end apart: 4, of which 3 were waited for; matrix products, arithmetic and copies ran while one was open for 0% of the time, Pallas kernels for 1%

profile of v4, /device:TPU:1, one launch (start us, length us, event | category | flops | bytes accessed | tf_op | source)
XLA Modules:
  0.0 79.6 jit_solution(11722880458217719883)
XLA Ops:
  0.0 3.2 %factors.1 = (bf16[128,2,1152]{2,1,0:T(2,128)(2,1)}, bf16[1152,128]{1,0:T(8,128)(2,1)}) custom-call(bf16[1152,128]{1,0:T(8,128)(2,1)} %bitcast.9, s32[24,48]{1,0:T(8,128)} %bitcast.10, f32[1,128]{1,0:T(1,128)} %bitcast.11, f32[1,128]{1,0:T(1,128)} %bitcast.12, bf16[128,512]{1,0:T(8,128)(2,1)} %refs_4_.1), custom_call_target="tpu_custom_call" | custom-call | tf_op jit(solution)/shard_map/factors/pallas_call | solution.py:204
  3.2 0.0 copy-start
  3.3 19.4 %all-to-all-start = ((bf16[128,2,1152]{2,1,0:T(2,128)(2,1)}), bf16[128,2,1152]{2,1,0:T(2,128)(2,1)S(1)}, u32[]{:S(2)}, u32[]{:S(2)}) async-start(bf16[128,2,1152]{2,1,0:T(2,128)(2,1)} %get-tuple-element.23), calls=%async_computation | async-start | bytes 1179648 | tf_op jit(solution)/shard_map/all_to_all | solution.py:223
  22.7 0.0 copy-start.3
  22.7 0.6 copy-done.3
  23.4 0.1 copy.10.rest_refs_0_
  23.5 0.0 copy-start.4
  23.5 0.7 copy-done.4
  24.1 0.0 copy-start.1
  24.1 0.0 copy-start.2
  24.1 0.1 copy.11.rest_refs_1_
  24.2 0.0 copy-done
  24.2 0.6 copy-done.1
  24.9 0.0 copy-done.2
  24.9 0.2 gate.1
  25.1 16.8 %all-to-all-done.x_ref = bf16[128,2,1152]{2,1,0:T(2,128)(2,1)S(1)} async-done(((bf16[128,2,1152]{2,1,0:T(2,128)(2,1)}), bf16[128,2,1152]{2,1,0:T(2,128)(2,1)S(1)}, u32[]{:S(2)}, u32[]{:S(2)}) %all-to-all-start) | async-done | bytes 589856 | tf_op jit(solution)/shard_map/all_to_all | solution.py:223
  41.9 0.5 right.1
  42.5 3.7 %collective-permute-start.2 = (bf16[192,384]{1,0:T(8,128)(2,1)S(1)}, bf16[192,384]{1,0:T(8,128)(2,1)S(1)}, u32[]{:S(2)}, u32[]{:S(2)}) collective-permute-start(bf16[192,384]{1,0:T(8,128)(2,1)S(1)} %get-tuple-element.26.keep_ref), channel_id=1, source_target_pairs={{0,96},{1,97},{2,98},{3,99},{4,100},{5,101},{6,102},{7,103},{8,104... | collective-permute-start | bytes 442376 | tf_op jit(solution)/shard_map/ppermute | solution.py:236
  46.2 0.3 left.1.bundle_ref
  46.5 5.5 %collective-permute-start.1 = (bf16[192,384]{1,0:T(8,128)(2,1)S(1)}, bf16[192,384]{1,0:T(8,128)(2,1)S(1)}, u32[]{:S(2)}, u32[]{:S(2)}) collective-permute-start(bf16[192,384]{1,0:T(8,128)(2,1)S(1)} %get-tuple-element.25.away_ref), channel_id=1, source_target_pairs={{0,97},{1,96},{2,99},{3,98},{4,101},{5,100},{6,103},{7,102},{8,105... | collective-permute-start | bytes 442376 | tf_op jit(solution)/shard_map/ppermute | solution.py:237
  52.1 1.9 %collective-permute-start = (bf16[576,384]{1,0:T(8,128)(2,1)S(1)}, bf16[576,384]{1,0:T(8,128)(2,1)S(1)}, u32[]{:S(2)}, u32[]{:S(2)}) collective-permute-start(bf16[576,384]{1,0:T(8,128)(2,1)S(1)} %left.1.bundle_ref), channel_id=1, source_target_pairs={{0,1},{1,0},{2,3},{3,2},{4,5},{5,4},{6,7},{7,6},{8,9},{9,8},{10,11... | collective-permute-start | bytes 1327112 | tf_op jit(solution)/shard_map/ppermute | solution.py:239
  54.0 0.0 collective-permute-done.2.mirror_ref
  54.0 0.5 own.1.own_ref
  54.6 0.6 collective-permute-done.1.cross_ref
  55.2 0.6 collective-permute-done.bundle_ref
  55.8 0.8 %contract.1 = bf16[128,2,624]{2,1,0:T(2,128)(2,1)S(1)} custom-call(bf16[576,384]{1,0:T(8,128)(2,1)S(1)} %collective-permute-done.bundle_ref, bf16[192,384]{1,0:T(8,128)(2,1)S(1)} %collective-permute-done.1.cross_ref, f32[3,384,128]{2,1,0:T(8,128)S(1)} %own.1.own_ref, s32[1]{0:T(128)} %bitcast.7.side_ref), custom_call_target="tpu_custom_call" | custom-call | tf_op jit(solution)/shard_map/contract/pallas_call | solution.py:248
  56.6 21.5 %all_to_all.10.x_ref = bf16[128,2,624]{2,1,0:T(2,128)(2,1)S(1)} all-to-all(bf16[128,2,624]{2,1,0:T(2,128)(2,1)S(1)} %contract.1), channel_id=1, replica_groups={{0,2,4,6,8,10,12,14,16,18,20,22,24,26,28,30,32,34,36,38,40,42,44,46,48,..., dimensions={0} | all-to-all | bytes 638976 | tf_op jit(solution)/shard_map/all_to_all | solution.py:256
  78.1 1.5 %update.1 = bf16[1152,128]{1,0:T(8,128)(2,1)} custom-call(bf16[128,2,624]{2,1,0:T(2,128)(2,1)S(1)} %all_to_all.10.x_ref, f32[1152,128]{1,0:T(8,128)S(1)} %get-tuple-element.27.gate_ref, f32[128,1]{1,0:T(8,128)S(1)} %get-tuple-element.28.gain_ref, f32[128,1]{1,0:T(8,128)S(1)} %get-tuple-element.29.bias_ref, bf16[128,128]{1,0:T(8,128)(2,1)S(1)} %get-tuple-element.30.w_ref), custom_call_target="tpu_custom_call" | custom-call | tf_op jit(solution)/shard_map/update/pallas_call | solution.py:257
Async XLA Ops:
  3.2 21.0 %copy-start = (bf16[1152,128]{1,0:T(8,128)(2,1)S(1)}, bf16[1152,128]{1,0:T(8,128)(2,1)}, u32[]{:S(2)}) copy-start(bf16[1152,128]{1,0:T(8,128)(2,1)} %get-tuple-element.18.normed_ref) | copy-start | bytes 884740
  3.3 38.7 %all-to-all-start = ((bf16[128,2,1152]{2,1,0:T(2,128)(2,1)}), bf16[128,2,1152]{2,1,0:T(2,128)(2,1)S(1)}, u32[]{:S(2)}, u32[]{:S(2)}) async-start(bf16[128,2,1152]{2,1,0:T(2,128)(2,1)} %get-tuple-element.23), calls=%async_computation | async-start | bytes 1179648 | tf_op jit(solution)/shard_map/all_to_all | solution.py:223
  22.7 0.7 copy-start.3
  23.5 0.7 copy-start.4
  24.1 0.8 copy-start.1
  24.1 0.8 copy-start.2
  42.5 11.5 %collective-permute-start.2 = (bf16[192,384]{1,0:T(8,128)(2,1)S(1)}, bf16[192,384]{1,0:T(8,128)(2,1)S(1)}, u32[]{:S(2)}, u32[]{:S(2)}) collective-permute-start(bf16[192,384]{1,0:T(8,128)(2,1)S(1)} %get-tuple-element.26.keep_ref), channel_id=1, source_target_pairs={{0,96},{1,97},{2,98},{3,99},{4,100},{5,101},{6,102},{7,103},{8,104... | collective-permute-start | bytes 442376 | tf_op jit(solution)/shard_map/ppermute | solution.py:236
  46.5 8.7 %collective-permute-start.1 = (bf16[192,384]{1,0:T(8,128)(2,1)S(1)}, bf16[192,384]{1,0:T(8,128)(2,1)S(1)}, u32[]{:S(2)}, u32[]{:S(2)}) collective-permute-start(bf16[192,384]{1,0:T(8,128)(2,1)S(1)} %get-tuple-element.25.away_ref), channel_id=1, source_target_pairs={{0,97},{1,96},{2,99},{3,98},{4,101},{5,100},{6,103},{7,102},{8,105... | collective-permute-start | bytes 442376 | tf_op jit(solution)/shard_map/ppermute | solution.py:237
  52.1 3.7 %collective-permute-start = (bf16[576,384]{1,0:T(8,128)(2,1)S(1)}, bf16[576,384]{1,0:T(8,128)(2,1)S(1)}, u32[]{:S(2)}, u32[]{:S(2)}) collective-permute-start(bf16[576,384]{1,0:T(8,128)(2,1)S(1)} %left.1.bundle_ref), channel_id=1, source_target_pairs={{0,1},{1,0},{2,3},{3,2},{4,5},{5,4},{6,7},{7,6},{8,9},{9,8},{10,11... | collective-permute-start | bytes 1327112 | tf_op jit(solution)/shard_map/ppermute | solution.py:239

commit v5 on v4

--- a/solution.py
+++ b/solution.py
@@ -32,8 +32,21 @@
     return x_low if side == 0 else 3 - x_low
 
 
+def lead(items, start):
+    return items[start:] + items[:start]
+
+
+ROW_ORDER = lead([(zh, xl) for zh in range(4) for xl in range(2)], 4)
+COL_ORDER = lead([(zl, y) for zl in range(2) for y in range(8)], 12)
+
+
 def positions():
-    return [(zh, xl, zl, y) for zh in range(4) for xl in range(2) for zl in range(2) for y in range(8)]
+    return [(zh, xl, zl, y) for zh, xl in ROW_ORDER for zl, y in COL_ORDER]
+
+
+def column_position(z_hi, x):
+    row = z_hi * 4 + x
+    return COL_ORDER.index((row // 8, row % 8))
 
 
 def channel_groups():
@@ -148,9 +161,9 @@
         part = jnp.zeros((JSPAN, SIDE), F32)
         for h in range(2):
             part += dot(right[:, h * JSPAN : (h + 1) * JSPAN], left[h * JSPAN : (h + 1) * JSPAN], ((0,), (0,)))
-        for rp in range(RPOS):
-            x = jnp.where(at == 0, rp % 2, 3 - rp % 2)
-            rows = pl.ds(pl.multiple_of(((rp // 2) * 4 + x) * COLS, 8), COLS)
+        for rp, (z_hi, x_low) in enumerate(ROW_ORDER):
+            places = [column_position(z_hi, x_of(s, x_low)) * COLS for s in range(2)]
+            rows = pl.ds(pl.multiple_of(jnp.where(at == 0, places[0], places[1]), 8), COLS)
             for t in range(SIDE // LANES):
                 piece = part[rp * COLS : (rp + 1) * COLS, t * LANES : (t + 1) * LANES]
                 total[t, rows, :] = piece if earlier is None else piece + earlier[t, rows, :]

time: 80.8 us -> 77.6 us (0.960); the launches traced: 79.6 us -> 77.3 us
  waiting for transfers between devices: 18 us -> 12.8 us
  blocking collectives: 21.5 us -> 23.3 us
  starting transfers between devices: 30.6 us -> 31.6 us
    all_to_all x1, waiting for transfers between devices: 16.8 us -> 11.6 us  [per_device(): both = exchange(send)]
    all_to_all x1, starting transfers between devices: 19.4 us -> 21.3 us  [per_device(): both = exchange(send)]
    all_to_all x1, blocking collectives: 21.5 us -> 23.3 us  [per_device(): combined = exchange(combined)]
    ppermute x1, starting transfers between devices: 5.54 us -> 4.67 us  [per_device(): cross = lax.ppermute(away, AXES, swap(True, True))]
where the time goes in v5:
time: 77.6 us; the launch traced here: 77.3 us
  starting transfers between devices  31.6 us (41%)
  blocking collectives  23.3 us (30%)
  waiting for transfers between devices  12.8 us (16%)
  Pallas kernels  7.19 us (9%)
  local copies, waits for them, and re-layouts  2.19 us (3%)
    all_to_all x1, blocking collectives, per_device(): combined = exchange(combined)  23.3 us
    all_to_all x1, starting transfers between devices, per_device(): both = exchange(send)  21.3 us
    all_to_all x1, waiting for transfers between devices, per_device(): both = exchange(send)  11.6 us
    ppermute x1, starting transfers between devices, per_device(): cross = lax.ppermute(away, AXES, swap(True, True))  4.67 us
    ppermute x1, starting transfers between devices, per_device(): mirror = lax.ppermute(keep, AXES, swap(True, False))  3.73 us
    pallas_call x1, Pallas kernels, per_device(): pl.pallas_call(factors_kernel, out_shape=(shape((WIDTH, 2, 2 * SPAN), BF1...  3.23 us
    unnamed x10, local copies, waits for them, and re-layouts  1.96 us
    ppermute x1, starting transfers between devices, per_device(): bundle_core = lax.ppermute(bundle, AXES, swap(False, True))  1.92 us
  transfers between devices with their start and end apart: 4, of which 3 were waited for; matrix products, arithmetic and copies ran while one was open for 0% of the time, Pallas kernels for 1%

profile of v5, /device:TPU:1, one launch (start us, length us, event | category | flops | bytes accessed | tf_op | source)
XLA Modules:
  0.0 77.3 jit_solution(16927414648091189922)
XLA Ops:
  0.0 3.2 %factors.1 = (bf16[128,2,1152]{2,1,0:T(2,128)(2,1)}, bf16[1152,128]{1,0:T(8,128)(2,1)}) custom-call(bf16[1152,128]{1,0:T(8,128)(2,1)} %bitcast.9, s32[24,48]{1,0:T(8,128)} %bitcast.10, f32[1,128]{1,0:T(1,128)} %bitcast.11, f32[1,128]{1,0:T(1,128)} %bitcast.12, bf16[128,512]{1,0:T(8,128)(2,1)} %refs_4_.1), custom_call_target="tpu_custom_call" | custom-call | tf_op jit(solution)/shard_map/factors/pallas_call | solution.py:217
  3.2 0.0 copy-start
  3.3 21.3 %all-to-all-start = ((bf16[128,2,1152]{2,1,0:T(2,128)(2,1)}), bf16[128,2,1152]{2,1,0:T(2,128)(2,1)S(1)}, u32[]{:S(2)}, u32[]{:S(2)}) async-start(bf16[128,2,1152]{2,1,0:T(2,128)(2,1)} %get-tuple-element.23), calls=%async_computation | async-start | bytes 1179648 | tf_op jit(solution)/shard_map/all_to_all | solution.py:236
  24.6 0.0 copy-start.3
  24.6 0.6 copy-done.3
  25.2 0.1 copy.10.rest_refs_0_
  25.3 0.0 copy-start.4
  25.4 0.7 copy-done.4
  26.0 0.0 copy-start.1
  26.0 0.0 copy-start.2
  26.0 0.1 copy.11.rest_refs_1_
  26.1 0.0 copy-done
  26.1 0.6 copy-done.1
  26.8 0.0 copy-done.2
  26.8 0.2 gate.1
  27.0 11.6 %all-to-all-done.x_ref = bf16[128,2,1152]{2,1,0:T(2,128)(2,1)S(1)} async-done(((bf16[128,2,1152]{2,1,0:T(2,128)(2,1)}), bf16[128,2,1152]{2,1,0:T(2,128)(2,1)S(1)}, u32[]{:S(2)}, u32[]{:S(2)}) %all-to-all-start) | async-done | bytes 589856 | tf_op jit(solution)/shard_map/all_to_all | solution.py:236
  38.7 0.5 right.1
  39.2 3.7 %collective-permute-start.2 = (bf16[192,384]{1,0:T(8,128)(2,1)S(1)}, bf16[192,384]{1,0:T(8,128)(2,1)S(1)}, u32[]{:S(2)}, u32[]{:S(2)}) collective-permute-start(bf16[192,384]{1,0:T(8,128)(2,1)S(1)} %get-tuple-element.26.keep_ref), channel_id=1, source_target_pairs={{0,96},{1,97},{2,98},{3,99},{4,100},{5,101},{6,102},{7,103},{8,104... | collective-permute-start | bytes 442376 | tf_op jit(solution)/shard_map/ppermute | solution.py:249
  43.0 0.3 left.1.bundle_ref
  43.3 4.7 %collective-permute-start.1 = (bf16[192,384]{1,0:T(8,128)(2,1)S(1)}, bf16[192,384]{1,0:T(8,128)(2,1)S(1)}, u32[]{:S(2)}, u32[]{:S(2)}) collective-permute-start(bf16[192,384]{1,0:T(8,128)(2,1)S(1)} %get-tuple-element.25.away_ref), channel_id=1, source_target_pairs={{0,97},{1,96},{2,99},{3,98},{4,101},{5,100},{6,103},{7,102},{8,105... | collective-permute-start | bytes 442376 | tf_op jit(solution)/shard_map/ppermute | solution.py:250
  47.9 1.9 %collective-permute-start = (bf16[576,384]{1,0:T(8,128)(2,1)S(1)}, bf16[576,384]{1,0:T(8,128)(2,1)S(1)}, u32[]{:S(2)}, u32[]{:S(2)}) collective-permute-start(bf16[576,384]{1,0:T(8,128)(2,1)S(1)} %left.1.bundle_ref), channel_id=1, source_target_pairs={{0,1},{1,0},{2,3},{3,2},{4,5},{5,4},{6,7},{7,6},{8,9},{9,8},{10,11... | collective-permute-start | bytes 1327112 | tf_op jit(solution)/shard_map/ppermute | solution.py:252
  49.9 0.0 collective-permute-done.2.mirror_ref
  49.9 0.5 own.1.own_ref
  50.4 1.0 %collective-permute-done.1.cross_ref = bf16[192,384]{1,0:T(8,128)(2,1)S(1)} collective-permute-done((bf16[192,384]{1,0:T(8,128)(2,1)S(1)}, bf16[192,384]{1,0:T(8,128)(2,1)S(1)}, u32[]{:S(2)}, u32[]{:S(2)}) %collective-permute-start.1) | collective-permute-done | bytes 147488 | tf_op jit(solution)/shard_map/ppermute | solution.py:250
  51.4 0.2 collective-permute-done.bundle_ref
  51.6 0.9 %contract.1 = bf16[128,2,624]{2,1,0:T(2,128)(2,1)S(1)} custom-call(bf16[576,384]{1,0:T(8,128)(2,1)S(1)} %collective-permute-done.bundle_ref, bf16[192,384]{1,0:T(8,128)(2,1)S(1)} %collective-permute-done.1.cross_ref, f32[3,384,128]{2,1,0:T(8,128)S(1)} %own.1.own_ref, s32[1]{0:T(128)} %bitcast.7.side_ref), custom_call_target="tpu_custom_call" | custom-call | tf_op jit(solution)/shard_map/contract/pallas_call | solution.py:261
  52.5 23.3 %all_to_all.10.x_ref = bf16[128,2,624]{2,1,0:T(2,128)(2,1)S(1)} all-to-all(bf16[128,2,624]{2,1,0:T(2,128)(2,1)S(1)} %contract.1), channel_id=1, replica_groups={{280,282,284,286,256,258,260,262,264,266,268,270,272,274,276,278,312,31..., dimensions={0} | all-to-all | bytes 638976 | tf_op jit(solution)/shard_map/all_to_all | solution.py:269
  75.8 1.5 %update.1 = bf16[1152,128]{1,0:T(8,128)(2,1)} custom-call(bf16[128,2,624]{2,1,0:T(2,128)(2,1)S(1)} %all_to_all.10.x_ref, f32[1152,128]{1,0:T(8,128)S(1)} %get-tuple-element.27.gate_ref, f32[128,1]{1,0:T(8,128)S(1)} %get-tuple-element.28.gain_ref, f32[128,1]{1,0:T(8,128)S(1)} %get-tuple-element.29.bias_ref, bf16[128,128]{1,0:T(8,128)(2,1)S(1)} %get-tuple-element.30.w_ref), custom_call_target="tpu_custom_call" | custom-call | tf_op jit(solution)/shard_map/update/pallas_call | solution.py:270
Async XLA Ops:
  3.2 22.9 %copy-start = (bf16[1152,128]{1,0:T(8,128)(2,1)S(1)}, bf16[1152,128]{1,0:T(8,128)(2,1)}, u32[]{:S(2)}) copy-start(bf16[1152,128]{1,0:T(8,128)(2,1)} %get-tuple-element.18.normed_ref) | copy-start | bytes 884740
  3.3 35.4 %all-to-all-start = ((bf16[128,2,1152]{2,1,0:T(2,128)(2,1)}), bf16[128,2,1152]{2,1,0:T(2,128)(2,1)S(1)}, u32[]{:S(2)}, u32[]{:S(2)}) async-start(bf16[128,2,1152]{2,1,0:T(2,128)(2,1)} %get-tuple-element.23), calls=%async_computation | async-start | bytes 1179648 | tf_op jit(solution)/shard_map/all_to_all | solution.py:236
  24.6 0.7 copy-start.3
  25.3 0.7 copy-start.4
  26.0 0.8 copy-start.1
  26.0 0.8 copy-start.2
  39.2 10.7 %collective-permute-start.2 = (bf16[192,384]{1,0:T(8,128)(2,1)S(1)}, bf16[192,384]{1,0:T(8,128)(2,1)S(1)}, u32[]{:S(2)}, u32[]{:S(2)}) collective-permute-start(bf16[192,384]{1,0:T(8,128)(2,1)S(1)} %get-tuple-element.26.keep_ref), channel_id=1, source_target_pairs={{0,96},{1,97},{2,98},{3,99},{4,100},{5,101},{6,102},{7,103},{8,104... | collective-permute-start | bytes 442376 | tf_op jit(solution)/shard_map/ppermute | solution.py:249
  43.3 8.2 %collective-permute-start.1 = (bf16[192,384]{1,0:T(8,128)(2,1)S(1)}, bf16[192,384]{1,0:T(8,128)(2,1)S(1)}, u32[]{:S(2)}, u32[]{:S(2)}) collective-permute-start(bf16[192,384]{1,0:T(8,128)(2,1)S(1)} %get-tuple-element.25.away_ref), channel_id=1, source_target_pairs={{0,97},{1,96},{2,99},{3,98},{4,101},{5,100},{6,103},{7,102},{8,105... | collective-permute-start | bytes 442376 | tf_op jit(solution)/shard_map/ppermute | solution.py:250
  47.9 3.7 %collective-permute-start = (bf16[576,384]{1,0:T(8,128)(2,1)S(1)}, bf16[576,384]{1,0:T(8,128)(2,1)S(1)}, u32[]{:S(2)}, u32[]{:S(2)}) collective-permute-start(bf16[576,384]{1,0:T(8,128)(2,1)S(1)} %left.1.bundle_ref), channel_id=1, source_target_pairs={{0,1},{1,0},{2,3},{3,2},{4,5},{5,4},{6,7},{7,6},{8,9},{9,8},{10,11... | collective-permute-start | bytes 1327112 | tf_op jit(solution)/shard_map/ppermute | solution.py:252

commit v6 on v5

--- a/solution.py
+++ b/solution.py
@@ -238,7 +238,6 @@
     late = call(
         gate_kernel, [shape((count, WIDTH), F32)] + [shape(value.shape, value.dtype) for value in last], name="gate"
     )(normed, gate_weight, *last)
-    late, both = lax.optimization_barrier((late, both))
     keep, away = pl.pallas_call(
         right_kernel,
         out_shape=(shape((JSPAN, SIDE), BF16),) * 2,
@@ -246,6 +245,7 @@
         compiler_params=pltpu.CompilerParams(vmem_limit_bytes=16 * 2**20),
         name="right",
     )(both, core)
+    late, keep = lax.optimization_barrier((late, keep))
     mirror = lax.ppermute(keep, AXES, swap(True, False))
     cross = lax.ppermute(away, AXES, swap(True, True))
     bundle = call(left_kernel, shape((SIDE + JSPAN, SIDE), BF16), name="left")(both, away)

time: 77.6 us -> 77.3 us (level)
  no operation moved by 1% of the time
where the time goes in v6:
time: 77.3 us; the launch traced here: 76.9 us
  starting transfers between devices  31.6 us (41%)
  blocking collectives  23 us (30%)
  waiting for transfers between devices  12.8 us (17%)
  Pallas kernels  7.19 us (9%)
  local copies, waits for them, and re-layouts  2.19 us (3%)
    all_to_all x1, blocking collectives, per_device(): combined = exchange(combined)  23 us
    all_to_all x1, starting transfers between devices, per_device(): both = exchange(send)  21.3 us
    all_to_all x1, waiting for transfers between devices, per_device(): both = exchange(send)  11.6 us
    ppermute x1, starting transfers between devices, per_device(): cross = lax.ppermute(away, AXES, swap(True, True))  4.67 us
    ppermute x1, starting transfers between devices, per_device(): mirror = lax.ppermute(keep, AXES, swap(True, False))  3.73 us
    pallas_call x1, Pallas kernels, per_device(): pl.pallas_call(factors_kernel, out_shape=(shape((WIDTH, 2, 2 * SPAN), BF1...  3.23 us
    unnamed x10, local copies, waits for them, and re-layouts  1.96 us
    ppermute x1, starting transfers between devices, per_device(): bundle_core = lax.ppermute(bundle, AXES, swap(False, True))  1.92 us
  transfers between devices with their start and end apart: 4, of which 3 were waited for; matrix products, arithmetic and copies ran while one was open for 0% of the time, Pallas kernels for 1%

profile of v6, /device:TPU:1, one launch (start us, length us, event | category | flops | bytes accessed | tf_op | source)
XLA Modules:
  0.0 76.9 jit_solution(16252297674955422377)
XLA Ops:
  0.0 3.2 %factors.1 = (bf16[128,2,1152]{2,1,0:T(2,128)(2,1)}, bf16[1152,128]{1,0:T(8,128)(2,1)}) custom-call(bf16[1152,128]{1,0:T(8,128)(2,1)} %bitcast.9, s32[24,48]{1,0:T(8,128)} %bitcast.10, f32[1,128]{1,0:T(1,128)} %bitcast.11, f32[1,128]{1,0:T(1,128)} %bitcast.12, bf16[128,512]{1,0:T(8,128)(2,1)} %refs_4_.1), custom_call_target="tpu_custom_call" | custom-call | tf_op jit(solution)/shard_map/factors/pallas_call | solution.py:217
  3.2 0.0 copy-start
  3.3 21.3 %all-to-all-start = ((bf16[128,2,1152]{2,1,0:T(2,128)(2,1)}), bf16[128,2,1152]{2,1,0:T(2,128)(2,1)S(1)}, u32[]{:S(2)}, u32[]{:S(2)}) async-start(bf16[128,2,1152]{2,1,0:T(2,128)(2,1)} %get-tuple-element.18), calls=%async_computation | async-start | bytes 1179648 | tf_op jit(solution)/shard_map/all_to_all | solution.py:236
  24.6 0.0 copy-start.3
  24.6 0.6 copy-done.3
  25.2 0.1 copy.10.rest_refs_0_
  25.3 0.0 copy-start.4
  25.4 0.7 copy-done.4
  26.0 0.0 copy-start.1
  26.0 0.0 copy-start.2
  26.0 0.1 copy.11.rest_refs_1_
  26.1 0.0 copy-done
  26.1 0.6 copy-done.1
  26.8 0.0 copy-done.2
  26.8 0.2 gate.1
  27.0 11.6 %all-to-all-done.x_ref = bf16[128,2,1152]{2,1,0:T(2,128)(2,1)S(1)} async-done(((bf16[128,2,1152]{2,1,0:T(2,128)(2,1)}), bf16[128,2,1152]{2,1,0:T(2,128)(2,1)S(1)}, u32[]{:S(2)}, u32[]{:S(2)}) %all-to-all-start) | async-done | bytes 589856 | tf_op jit(solution)/shard_map/all_to_all | solution.py:236
  38.7 0.5 right.1
  39.2 3.7 %collective-permute-start.2 = (bf16[192,384]{1,0:T(8,128)(2,1)S(1)}, bf16[192,384]{1,0:T(8,128)(2,1)S(1)}, u32[]{:S(2)}, u32[]{:S(2)}) collective-permute-start(bf16[192,384]{1,0:T(8,128)(2,1)S(1)} %get-tuple-element.26.keep_ref), channel_id=1, source_target_pairs={{0,96},{1,97},{2,98},{3,99},{4,100},{5,101},{6,102},{7,103},{8,104... | collective-permute-start | bytes 442376 | tf_op jit(solution)/shard_map/ppermute | solution.py:249
  43.0 4.7 %collective-permute-start.1 = (bf16[192,384]{1,0:T(8,128)(2,1)S(1)}, bf16[192,384]{1,0:T(8,128)(2,1)S(1)}, u32[]{:S(2)}, u32[]{:S(2)}) collective-permute-start(bf16[192,384]{1,0:T(8,128)(2,1)S(1)} %get-tuple-element.19.away_ref), channel_id=1, source_target_pairs={{0,97},{1,96},{2,99},{3,98},{4,101},{5,100},{6,103},{7,102},{8,105... | collective-permute-start | bytes 442376 | tf_op jit(solution)/shard_map/ppermute | solution.py:250
  47.6 0.3 left.1.bundle_ref
  47.9 1.9 %collective-permute-start = (bf16[576,384]{1,0:T(8,128)(2,1)S(1)}, bf16[576,384]{1,0:T(8,128)(2,1)S(1)}, u32[]{:S(2)}, u32[]{:S(2)}) collective-permute-start(bf16[576,384]{1,0:T(8,128)(2,1)S(1)} %left.1.bundle_ref), channel_id=1, source_target_pairs={{0,1},{1,0},{2,3},{3,2},{4,5},{5,4},{6,7},{7,6},{8,9},{9,8},{10,11... | collective-permute-start | bytes 1327112 | tf_op jit(solution)/shard_map/ppermute | solution.py:252
  49.9 0.0 collective-permute-done.2.mirror_ref
  49.9 0.5 own.1.own_ref
  50.4 0.7 collective-permute-done.1.cross_ref
  51.1 0.5 collective-permute-done.bundle_ref
  51.6 0.9 %contract.1 = bf16[128,2,624]{2,1,0:T(2,128)(2,1)S(1)} custom-call(bf16[576,384]{1,0:T(8,128)(2,1)S(1)} %collective-permute-done.bundle_ref, bf16[192,384]{1,0:T(8,128)(2,1)S(1)} %collective-permute-done.1.cross_ref, f32[3,384,128]{2,1,0:T(8,128)S(1)} %own.1.own_ref, s32[1]{0:T(128)} %bitcast.7.side_ref), custom_call_target="tpu_custom_call" | custom-call | tf_op jit(solution)/shard_map/contract/pallas_call | solution.py:261
  52.5 23.0 %all_to_all.10.x_ref = bf16[128,2,624]{2,1,0:T(2,128)(2,1)S(1)} all-to-all(bf16[128,2,624]{2,1,0:T(2,128)(2,1)S(1)} %contract.1), channel_id=1, replica_groups={{280,282,284,286,256,258,260,262,264,266,268,270,272,274,276,278,312,31..., dimensions={0} | all-to-all | bytes 638976 | tf_op jit(solution)/shard_map/all_to_all | solution.py:269
  75.5 1.5 %update.1 = bf16[1152,128]{1,0:T(8,128)(2,1)} custom-call(bf16[128,2,624]{2,1,0:T(2,128)(2,1)S(1)} %all_to_all.10.x_ref, f32[1152,128]{1,0:T(8,128)S(1)} %get-tuple-element.27.gate_ref, f32[128,1]{1,0:T(8,128)S(1)} %get-tuple-element.28.gain_ref, f32[128,1]{1,0:T(8,128)S(1)} %get-tuple-element.29.bias_ref, bf16[128,128]{1,0:T(8,128)(2,1)S(1)} %get-tuple-element.30.w_ref), custom_call_target="tpu_custom_call" | custom-call | tf_op jit(solution)/shard_map/update/pallas_call | solution.py:270
Async XLA Ops:
  3.2 22.9 %copy-start = (bf16[1152,128]{1,0:T(8,128)(2,1)S(1)}, bf16[1152,128]{1,0:T(8,128)(2,1)}, u32[]{:S(2)}) copy-start(bf16[1152,128]{1,0:T(8,128)(2,1)} %get-tuple-element.20.normed_ref) | copy-start | bytes 884740
  3.3 35.4 %all-to-all-start = ((bf16[128,2,1152]{2,1,0:T(2,128)(2,1)}), bf16[128,2,1152]{2,1,0:T(2,128)(2,1)S(1)}, u32[]{:S(2)}, u32[]{:S(2)}) async-start(bf16[128,2,1152]{2,1,0:T(2,128)(2,1)} %get-tuple-element.18), calls=%async_computation | async-start | bytes 1179648 | tf_op jit(solution)/shard_map/all_to_all | solution.py:236
  24.6 0.7 copy-start.3
  25.3 0.7 copy-start.4
  26.0 0.8 copy-start.1
  26.0 0.8 %copy-start.2 = (bf16[128,128]{1,0:T(8,128)(2,1)S(1)}, bf16[128,128]{1,0:T(8,128)(2,1)}, u32[]{:S(2)}) copy-start(bf16[128,128]{1,0:T(8,128)(2,1)} %rest_refs_2_.1) | copy-start | bytes 98308
  39.2 10.7 %collective-permute-start.2 = (bf16[192,384]{1,0:T(8,128)(2,1)S(1)}, bf16[192,384]{1,0:T(8,128)(2,1)S(1)}, u32[]{:S(2)}, u32[]{:S(2)}) collective-permute-start(bf16[192,384]{1,0:T(8,128)(2,1)S(1)} %get-tuple-element.26.keep_ref), channel_id=1, source_target_pairs={{0,96},{1,97},{2,98},{3,99},{4,100},{5,101},{6,102},{7,103},{8,104... | collective-permute-start | bytes 442376 | tf_op jit(solution)/shard_map/ppermute | solution.py:249
  43.0 8.2 %collective-permute-start.1 = (bf16[192,384]{1,0:T(8,128)(2,1)S(1)}, bf16[192,384]{1,0:T(8,128)(2,1)S(1)}, u32[]{:S(2)}, u32[]{:S(2)}) collective-permute-start(bf16[192,384]{1,0:T(8,128)(2,1)S(1)} %get-tuple-element.19.away_ref), channel_id=1, source_target_pairs={{0,97},{1,96},{2,99},{3,98},{4,101},{5,100},{6,103},{7,102},{8,105... | collective-permute-start | bytes 442376 | tf_op jit(solution)/shard_map/ppermute | solution.py:250
  47.9 3.7 %collective-permute-start = (bf16[576,384]{1,0:T(8,128)(2,1)S(1)}, bf16[576,384]{1,0:T(8,128)(2,1)S(1)}, u32[]{:S(2)}, u32[]{:S(2)}) collective-permute-start(bf16[576,384]{1,0:T(8,128)(2,1)S(1)} %left.1.bundle_ref), channel_id=1, source_target_pairs={{0,1},{1,0},{2,3},{3,2},{4,5},{5,4},{6,7},{7,6},{8,9},{9,8},{10,11... | collective-permute-start | bytes 1327112 | tf_op jit(solution)/shard_map/ppermute | solution.py:252

commit v7 on v6

--- a/solution.py
+++ b/solution.py
@@ -32,12 +32,20 @@
     return x_low if side == 0 else 3 - x_low
 
 
-def lead(items, start):
-    return items[start:] + items[:start]
-
-
-ROW_ORDER = lead([(zh, xl) for zh in range(4) for xl in range(2)], 4)
-COL_ORDER = lead([(zl, y) for zl in range(2) for y in range(8)], 12)
+def ring(a, b):
+    return min((a - b) % 8, (b - a) % 8)
+
+
+def from_far(items, first, distance):
+    return [first] + sorted([item for item in items if item != first], key=lambda item: -distance(item))
+
+
+ROW_ORDER = from_far(
+    [(zh, xl) for zh in range(4) for xl in range(2)], (2, 0), lambda place: ring(2 * place[0], 4) + place[1]
+)
+COL_ORDER = from_far(
+    [(zl, y) for zl in range(2) for y in range(8)], (1, 4), lambda place: ring(place[1], 4) + 1 - place[0]
+)
 
 
 def positions():

time: 77.3 us -> 75.4 us (0.975); the launches traced: 76.9 us -> 74.2 us
  blocking collectives: 23 us -> 20.8 us
    all_to_all x1, blocking collectives: 23 us -> 20.8 us  [per_device(): combined = exchange(combined)]
where the time goes in v7:
time: 75.4 us; the launch traced here: 74.2 us
  starting transfers between devices  31.7 us (42%)
  blocking collectives  20.8 us (28%)
  waiting for transfers between devices  12.2 us (16%)
  Pallas kernels  7.17 us (10%)
  local copies, waits for them, and re-layouts  2.19 us (3%)
    all_to_all x1, starting transfers between devices, per_device(): both = exchange(send)  21.1 us
    all_to_all x1, blocking collectives, per_device(): combined = exchange(combined)  20.8 us
    all_to_all x1, waiting for transfers between devices, per_device(): both = exchange(send)  11 us
    ppermute x1, starting transfers between devices, per_device(): cross = lax.ppermute(away, AXES, swap(True, True))  5.04 us
    ppermute x1, starting transfers between devices, per_device(): mirror = lax.ppermute(keep, AXES, swap(True, False))  3.71 us
    pallas_call x1, Pallas kernels, per_device(): pl.pallas_call(factors_kernel, out_shape=(shape((WIDTH, 2, 2 * SPAN), BF1...  3.23 us
    unnamed x10, local copies, waits for them, and re-layouts  1.96 us
    ppermute x1, starting transfers between devices, per_device(): bundle_core = lax.ppermute(bundle, AXES, swap(False, True))  1.92 us
  transfers between devices with their start and end apart: 4, of which 3 were waited for; matrix products, arithmetic and copies ran while one was open for 0% of the time, Pallas kernels for 1%

profile of v7, /device:TPU:1, one launch (start us, length us, event | category | flops | bytes accessed | tf_op | source)
XLA Modules:
  0.0 74.2 jit_solution(909905280234947837)
XLA Ops:
  0.0 3.2 %factors.1 = (bf16[128,2,1152]{2,1,0:T(2,128)(2,1)}, bf16[1152,128]{1,0:T(8,128)(2,1)}) custom-call(bf16[1152,128]{1,0:T(8,128)(2,1)} %bitcast.9, s32[24,48]{1,0:T(8,128)} %bitcast.10, f32[1,128]{1,0:T(1,128)} %bitcast.11, f32[1,128]{1,0:T(1,128)} %bitcast.12, bf16[128,512]{1,0:T(8,128)(2,1)} %refs_4_.1), custom_call_target="tpu_custom_call" | custom-call | tf_op jit(solution)/shard_map/factors/pallas_call | solution.py:225
  3.2 0.0 copy-start
  3.3 21.1 %all-to-all-start = ((bf16[128,2,1152]{2,1,0:T(2,128)(2,1)}), bf16[128,2,1152]{2,1,0:T(2,128)(2,1)S(1)}, u32[]{:S(2)}, u32[]{:S(2)}) async-start(bf16[128,2,1152]{2,1,0:T(2,128)(2,1)} %get-tuple-element.18), calls=%async_computation | async-start | bytes 1179648 | tf_op jit(solution)/shard_map/all_to_all | solution.py:244
  24.3 0.0 copy-start.3
  24.3 0.6 copy-done.3
  25.0 0.1 copy.10.rest_refs_0_
  25.1 0.0 copy-start.4
  25.1 0.7 copy-done.4
  25.8 0.0 copy-start.1
  25.8 0.0 copy-start.2
  25.8 0.1 copy.11.rest_refs_1_
  25.9 0.0 copy-done
  25.9 0.6 copy-done.1
  26.5 0.0 copy-done.2
  26.5 0.2 gate.1
  26.8 11.0 %all-to-all-done.x_ref = bf16[128,2,1152]{2,1,0:T(2,128)(2,1)S(1)} async-done(((bf16[128,2,1152]{2,1,0:T(2,128)(2,1)}), bf16[128,2,1152]{2,1,0:T(2,128)(2,1)S(1)}, u32[]{:S(2)}, u32[]{:S(2)}) %all-to-all-start) | async-done | bytes 589856 | tf_op jit(solution)/shard_map/all_to_all | solution.py:244
  37.8 0.5 right.1
  38.3 3.7 %collective-permute-start.2 = (bf16[192,384]{1,0:T(8,128)(2,1)S(1)}, bf16[192,384]{1,0:T(8,128)(2,1)S(1)}, u32[]{:S(2)}, u32[]{:S(2)}) collective-permute-start(bf16[192,384]{1,0:T(8,128)(2,1)S(1)} %get-tuple-element.26.keep_ref), channel_id=1, source_target_pairs={{0,96},{1,97},{2,98},{3,99},{4,100},{5,101},{6,102},{7,103},{8,104... | collective-permute-start | bytes 442376 | tf_op jit(solution)/shard_map/ppermute | solution.py:257
  42.0 5.0 %collective-permute-start.1 = (bf16[192,384]{1,0:T(8,128)(2,1)S(1)}, bf16[192,384]{1,0:T(8,128)(2,1)S(1)}, u32[]{:S(2)}, u32[]{:S(2)}) collective-permute-start(bf16[192,384]{1,0:T(8,128)(2,1)S(1)} %get-tuple-element.19.away_ref), channel_id=1, source_target_pairs={{0,97},{1,96},{2,99},{3,98},{4,101},{5,100},{6,103},{7,102},{8,105... | collective-permute-start | bytes 442376 | tf_op jit(solution)/shard_map/ppermute | solution.py:258
  47.1 0.3 left.1.bundle_ref
  47.4 1.9 %collective-permute-start = (bf16[576,384]{1,0:T(8,128)(2,1)S(1)}, bf16[576,384]{1,0:T(8,128)(2,1)S(1)}, u32[]{:S(2)}, u32[]{:S(2)}) collective-permute-start(bf16[576,384]{1,0:T(8,128)(2,1)S(1)} %left.1.bundle_ref), channel_id=1, source_target_pairs={{0,1},{1,0},{2,3},{3,2},{4,5},{5,4},{6,7},{7,6},{8,9},{9,8},{10,11... | collective-permute-start | bytes 1327112 | tf_op jit(solution)/shard_map/ppermute | solution.py:260
  49.3 0.0 collective-permute-done.2.mirror_ref
  49.3 0.5 own.1.own_ref
  49.9 0.3 collective-permute-done.1.cross_ref
  50.2 0.9 %collective-permute-done.bundle_ref = bf16[576,384]{1,0:T(8,128)(2,1)S(1)} collective-permute-done((bf16[576,384]{1,0:T(8,128)(2,1)S(1)}, bf16[576,384]{1,0:T(8,128)(2,1)S(1)}, u32[]{:S(2)}, u32[]{:S(2)}) %collective-permute-start) | collective-permute-done | bytes 442400 | tf_op jit(solution)/shard_map/ppermute | solution.py:260
  51.1 0.8 %contract.1 = bf16[128,2,624]{2,1,0:T(2,128)(2,1)S(1)} custom-call(bf16[576,384]{1,0:T(8,128)(2,1)S(1)} %collective-permute-done.bundle_ref, bf16[192,384]{1,0:T(8,128)(2,1)S(1)} %collective-permute-done.1.cross_ref, f32[3,384,128]{2,1,0:T(8,128)S(1)} %own.1.own_ref, s32[1]{0:T(128)} %bitcast.7.side_ref), custom_call_target="tpu_custom_call" | custom-call | tf_op jit(solution)/shard_map/contract/pallas_call | solution.py:269
  51.9 20.8 %all_to_all.10.x_ref = bf16[128,2,624]{2,1,0:T(2,128)(2,1)S(1)} all-to-all(bf16[128,2,624]{2,1,0:T(2,128)(2,1)S(1)} %contract.1), channel_id=1, replica_groups={{280,256,258,270,272,260,268,274,286,262,266,276,284,264,278,282,56,32,..., dimensions={0} | all-to-all | bytes 638976 | tf_op jit(solution)/shard_map/all_to_all | solution.py:277
  72.7 1.5 %update.1 = bf16[1152,128]{1,0:T(8,128)(2,1)} custom-call(bf16[128,2,624]{2,1,0:T(2,128)(2,1)S(1)} %all_to_all.10.x_ref, f32[1152,128]{1,0:T(8,128)S(1)} %get-tuple-element.27.gate_ref, f32[128,1]{1,0:T(8,128)S(1)} %get-tuple-element.28.gain_ref, f32[128,1]{1,0:T(8,128)S(1)} %get-tuple-element.29.bias_ref, bf16[128,128]{1,0:T(8,128)(2,1)S(1)} %get-tuple-element.30.w_ref), custom_call_target="tpu_custom_call" | custom-call | tf_op jit(solution)/shard_map/update/pallas_call | solution.py:278
Async XLA Ops:
  3.2 22.6 %copy-start = (bf16[1152,128]{1,0:T(8,128)(2,1)S(1)}, bf16[1152,128]{1,0:T(8,128)(2,1)}, u32[]{:S(2)}) copy-start(bf16[1152,128]{1,0:T(8,128)(2,1)} %get-tuple-element.20.normed_ref) | copy-start | bytes 884740
  3.3 34.5 %all-to-all-start = ((bf16[128,2,1152]{2,1,0:T(2,128)(2,1)}), bf16[128,2,1152]{2,1,0:T(2,128)(2,1)S(1)}, u32[]{:S(2)}, u32[]{:S(2)}) async-start(bf16[128,2,1152]{2,1,0:T(2,128)(2,1)} %get-tuple-element.18), calls=%async_computation | async-start | bytes 1179648 | tf_op jit(solution)/shard_map/all_to_all | solution.py:244
  24.3 0.7 copy-start.3
  25.1 0.7 copy-start.4
  25.8 0.8 %copy-start.1 = (bf16[128,128]{1,0:T(8,128)(2,1)S(1)}, bf16[128,128]{1,0:T(8,128)(2,1)}, u32[]{:S(2)}) copy-start(bf16[128,128]{1,0:T(8,128)(2,1)} %w_ref.1) | copy-start | bytes 98308
  25.8 0.8 %copy-start.2 = (bf16[128,128]{1,0:T(8,128)(2,1)S(1)}, bf16[128,128]{1,0:T(8,128)(2,1)}, u32[]{:S(2)}) copy-start(bf16[128,128]{1,0:T(8,128)(2,1)} %rest_refs_2_.1) | copy-start | bytes 98308
  38.3 11.0 %collective-permute-start.2 = (bf16[192,384]{1,0:T(8,128)(2,1)S(1)}, bf16[192,384]{1,0:T(8,128)(2,1)S(1)}, u32[]{:S(2)}, u32[]{:S(2)}) collective-permute-start(bf16[192,384]{1,0:T(8,128)(2,1)S(1)} %get-tuple-element.26.keep_ref), channel_id=1, source_target_pairs={{0,96},{1,97},{2,98},{3,99},{4,100},{5,101},{6,102},{7,103},{8,104... | collective-permute-start | bytes 442376 | tf_op jit(solution)/shard_map/ppermute | solution.py:257
  42.0 8.2 %collective-permute-start.1 = (bf16[192,384]{1,0:T(8,128)(2,1)S(1)}, bf16[192,384]{1,0:T(8,128)(2,1)S(1)}, u32[]{:S(2)}, u32[]{:S(2)}) collective-permute-start(bf16[192,384]{1,0:T(8,128)(2,1)S(1)} %get-tuple-element.19.away_ref), channel_id=1, source_target_pairs={{0,97},{1,96},{2,99},{3,98},{4,101},{5,100},{6,103},{7,102},{8,105... | collective-permute-start | bytes 442376 | tf_op jit(solution)/shard_map/ppermute | solution.py:258
  47.4 3.7 %collective-permute-start = (bf16[576,384]{1,0:T(8,128)(2,1)S(1)}, bf16[576,384]{1,0:T(8,128)(2,1)S(1)}, u32[]{:S(2)}, u32[]{:S(2)}) collective-permute-start(bf16[576,384]{1,0:T(8,128)(2,1)S(1)} %left.1.bundle_ref), channel_id=1, source_target_pairs={{0,1},{1,0},{2,3},{3,2},{4,5},{5,4},{6,7},{7,6},{8,9},{9,8},{10,11... | collective-permute-start | bytes 1327112 | tf_op jit(solution)/shard_map/ppermute | solution.py:260

commit v8 on v7

--- a/solution.py
+++ b/solution.py
@@ -41,7 +41,7 @@
 
 
 ROW_ORDER = from_far(
-    [(zh, xl) for zh in range(4) for xl in range(2)], (2, 0), lambda place: ring(2 * place[0], 4) + place[1]
+    [(zh, xl) for zh in range(4) for xl in range(2)], (2, 0), lambda place: (ring(2 * place[0], 5) + ring(2 * place[0] + 1, 5)) / 2 + place[1]
 )
 COL_ORDER = from_far(
     [(zl, y) for zl in range(2) for y in range(8)], (1, 4), lambda place: ring(place[1], 4) + 1 - place[0]

time: 75.4 us -> 75 us (level)
  no operation moved by 1% of the time
where the time goes in v8:
time: 75 us; the launch traced here: 74 us
  starting transfers between devices  31.5 us (42%)
  blocking collectives  20.6 us (27%)
  waiting for transfers between devices  12.5 us (17%)
  Pallas kernels  7.17 us (10%)
  local copies, waits for them, and re-layouts  2.19 us (3%)
    all_to_all x1, starting transfers between devices, per_device(): both = exchange(send)  21.1 us
    all_to_all x1, blocking collectives, per_device(): combined = exchange(combined)  20.6 us
    all_to_all x1, waiting for transfers between devices, per_device(): both = exchange(send)  11.3 us
    ppermute x1, starting transfers between devices, per_device(): cross = lax.ppermute(away, AXES, swap(True, True))  4.74 us
    ppermute x1, starting transfers between devices, per_device(): mirror = lax.ppermute(keep, AXES, swap(True, False))  3.72 us
    pallas_call x1, Pallas kernels, per_device(): pl.pallas_call(factors_kernel, out_shape=(shape((WIDTH, 2, 2 * SPAN), BF1...  3.23 us
    unnamed x10, local copies, waits for them, and re-layouts  1.96 us
    ppermute x1, starting transfers between devices, per_device(): bundle_core = lax.ppermute(bundle, AXES, swap(False, True))  1.92 us
  transfers between devices with their start and end apart: 4, of which 3 were waited for; matrix products, arithmetic and copies ran while one was open for 0% of the time, Pallas kernels for 1%

profile of v8, /device:TPU:1, one launch (start us, length us, event | category | flops | bytes accessed | tf_op | source)
XLA Modules:
  0.0 74.0 jit_solution(16563488686864832657)
XLA Ops:
  0.0 3.2 %factors.1 = (bf16[128,2,1152]{2,1,0:T(2,128)(2,1)}, bf16[1152,128]{1,0:T(8,128)(2,1)}) custom-call(bf16[1152,128]{1,0:T(8,128)(2,1)} %bitcast.9, s32[24,48]{1,0:T(8,128)} %bitcast.10, f32[1,128]{1,0:T(1,128)} %bitcast.11, f32[1,128]{1,0:T(1,128)} %bitcast.12, bf16[128,512]{1,0:T(8,128)(2,1)} %refs_4_.1), custom_call_target="tpu_custom_call" | custom-call | tf_op jit(solution)/shard_map/factors/pallas_call | solution.py:225
  3.2 0.0 copy-start
  3.3 21.1 %all-to-all-start = ((bf16[128,2,1152]{2,1,0:T(2,128)(2,1)}), bf16[128,2,1152]{2,1,0:T(2,128)(2,1)S(1)}, u32[]{:S(2)}, u32[]{:S(2)}) async-start(bf16[128,2,1152]{2,1,0:T(2,128)(2,1)} %get-tuple-element.18), calls=%async_computation | async-start | bytes 1179648 | tf_op jit(solution)/shard_map/all_to_all | solution.py:244
  24.3 0.0 copy-start.3
  24.3 0.6 copy-done.3
  25.0 0.1 copy.10.rest_refs_0_
  25.1 0.0 copy-start.4
  25.1 0.7 copy-done.4
  25.8 0.0 copy-start.1
  25.8 0.0 copy-start.2
  25.8 0.1 copy.11.rest_refs_1_
  25.9 0.0 copy-done
  25.9 0.6 copy-done.1
  26.5 0.0 copy-done.2
  26.5 0.2 gate.1
  26.8 11.3 %all-to-all-done.x_ref = bf16[128,2,1152]{2,1,0:T(2,128)(2,1)S(1)} async-done(((bf16[128,2,1152]{2,1,0:T(2,128)(2,1)}), bf16[128,2,1152]{2,1,0:T(2,128)(2,1)S(1)}, u32[]{:S(2)}, u32[]{:S(2)}) %all-to-all-start) | async-done | bytes 589856 | tf_op jit(solution)/shard_map/all_to_all | solution.py:244
  38.1 0.5 right.1
  38.6 3.7 %collective-permute-start.2 = (bf16[192,384]{1,0:T(8,128)(2,1)S(1)}, bf16[192,384]{1,0:T(8,128)(2,1)S(1)}, u32[]{:S(2)}, u32[]{:S(2)}) collective-permute-start(bf16[192,384]{1,0:T(8,128)(2,1)S(1)} %get-tuple-element.26.keep_ref), channel_id=1, source_target_pairs={{0,96},{1,97},{2,98},{3,99},{4,100},{5,101},{6,102},{7,103},{8,104... | collective-permute-start | bytes 442376 | tf_op jit(solution)/shard_map/ppermute | solution.py:257
  42.4 4.7 %collective-permute-start.1 = (bf16[192,384]{1,0:T(8,128)(2,1)S(1)}, bf16[192,384]{1,0:T(8,128)(2,1)S(1)}, u32[]{:S(2)}, u32[]{:S(2)}) collective-permute-start(bf16[192,384]{1,0:T(8,128)(2,1)S(1)} %get-tuple-element.19.away_ref), channel_id=1, source_target_pairs={{0,97},{1,96},{2,99},{3,98},{4,101},{5,100},{6,103},{7,102},{8,105... | collective-permute-start | bytes 442376 | tf_op jit(solution)/shard_map/ppermute | solution.py:258
  47.1 0.3 left.1.bundle_ref
  47.4 1.9 %collective-permute-start = (bf16[576,384]{1,0:T(8,128)(2,1)S(1)}, bf16[576,384]{1,0:T(8,128)(2,1)S(1)}, u32[]{:S(2)}, u32[]{:S(2)}) collective-permute-start(bf16[576,384]{1,0:T(8,128)(2,1)S(1)} %left.1.bundle_ref), channel_id=1, source_target_pairs={{0,1},{1,0},{2,3},{3,2},{4,5},{5,4},{6,7},{7,6},{8,9},{9,8},{10,11... | collective-permute-start | bytes 1327112 | tf_op jit(solution)/shard_map/ppermute | solution.py:260
  49.4 0.0 collective-permute-done.2.mirror_ref
  49.4 0.5 own.1.own_ref
  49.9 0.5 collective-permute-done.1.cross_ref
  50.5 0.7 collective-permute-done.bundle_ref
  51.1 0.8 %contract.1 = bf16[128,2,624]{2,1,0:T(2,128)(2,1)S(1)} custom-call(bf16[576,384]{1,0:T(8,128)(2,1)S(1)} %collective-permute-done.bundle_ref, bf16[192,384]{1,0:T(8,128)(2,1)S(1)} %collective-permute-done.1.cross_ref, f32[3,384,128]{2,1,0:T(8,128)S(1)} %own.1.own_ref, s32[1]{0:T(128)} %bitcast.7.side_ref), custom_call_target="tpu_custom_call" | custom-call | tf_op jit(solution)/shard_map/contract/pallas_call | solution.py:269
  52.0 20.6 %all_to_all.10.x_ref = bf16[128,2,624]{2,1,0:T(2,128)(2,1)S(1)} all-to-all(bf16[128,2,624]{2,1,0:T(2,128)(2,1)S(1)} %contract.1), channel_id=1, replica_groups={{280,256,258,270,272,260,268,274,286,262,266,276,284,264,278,282,56,32,..., dimensions={0} | all-to-all | bytes 638976 | tf_op jit(solution)/shard_map/all_to_all | solution.py:277
  72.5 1.5 %update.1 = bf16[1152,128]{1,0:T(8,128)(2,1)} custom-call(bf16[128,2,624]{2,1,0:T(2,128)(2,1)S(1)} %all_to_all.10.x_ref, f32[1152,128]{1,0:T(8,128)S(1)} %get-tuple-element.27.gate_ref, f32[128,1]{1,0:T(8,128)S(1)} %get-tuple-element.28.gain_ref, f32[128,1]{1,0:T(8,128)S(1)} %get-tuple-element.29.bias_ref, bf16[128,128]{1,0:T(8,128)(2,1)S(1)} %get-tuple-element.30.w_ref), custom_call_target="tpu_custom_call" | custom-call | tf_op jit(solution)/shard_map/update/pallas_call | solution.py:278
Async XLA Ops:
  3.2 22.6 %copy-start = (bf16[1152,128]{1,0:T(8,128)(2,1)S(1)}, bf16[1152,128]{1,0:T(8,128)(2,1)}, u32[]{:S(2)}) copy-start(bf16[1152,128]{1,0:T(8,128)(2,1)} %get-tuple-element.20.normed_ref) | copy-start | bytes 884740
  3.3 34.8 %all-to-all-start = ((bf16[128,2,1152]{2,1,0:T(2,128)(2,1)}), bf16[128,2,1152]{2,1,0:T(2,128)(2,1)S(1)}, u32[]{:S(2)}, u32[]{:S(2)}) async-start(bf16[128,2,1152]{2,1,0:T(2,128)(2,1)} %get-tuple-element.18), calls=%async_computation | async-start | bytes 1179648 | tf_op jit(solution)/shard_map/all_to_all | solution.py:244
  24.3 0.7 copy-start.3
  25.1 0.7 copy-start.4
  25.8 0.8 %copy-start.1 = (bf16[128,128]{1,0:T(8,128)(2,1)S(1)}, bf16[128,128]{1,0:T(8,128)(2,1)}, u32[]{:S(2)}) copy-start(bf16[128,128]{1,0:T(8,128)(2,1)} %w_ref.1) | copy-start | bytes 98308
  25.8 0.8 %copy-start.2 = (bf16[128,128]{1,0:T(8,128)(2,1)S(1)}, bf16[128,128]{1,0:T(8,128)(2,1)}, u32[]{:S(2)}) copy-start(bf16[128,128]{1,0:T(8,128)(2,1)} %rest_refs_2_.1) | copy-start | bytes 98308
  38.6 10.8 %collective-permute-start.2 = (bf16[192,384]{1,0:T(8,128)(2,1)S(1)}, bf16[192,384]{1,0:T(8,128)(2,1)S(1)}, u32[]{:S(2)}, u32[]{:S(2)}) collective-permute-start(bf16[192,384]{1,0:T(8,128)(2,1)S(1)} %get-tuple-element.26.keep_ref), channel_id=1, source_target_pairs={{0,96},{1,97},{2,98},{3,99},{4,100},{5,101},{6,102},{7,103},{8,104... | collective-permute-start | bytes 442376 | tf_op jit(solution)/shard_map/ppermute | solution.py:257
  42.4 8.1 %collective-permute-start.1 = (bf16[192,384]{1,0:T(8,128)(2,1)S(1)}, bf16[192,384]{1,0:T(8,128)(2,1)S(1)}, u32[]{:S(2)}, u32[]{:S(2)}) collective-permute-start(bf16[192,384]{1,0:T(8,128)(2,1)S(1)} %get-tuple-element.19.away_ref), channel_id=1, source_target_pairs={{0,97},{1,96},{2,99},{3,98},{4,101},{5,100},{6,103},{7,102},{8,105... | collective-permute-start | bytes 442376 | tf_op jit(solution)/shard_map/ppermute | solution.py:258
  47.4 3.7 %collective-permute-start = (bf16[576,384]{1,0:T(8,128)(2,1)S(1)}, bf16[576,384]{1,0:T(8,128)(2,1)S(1)}, u32[]{:S(2)}, u32[]{:S(2)}) collective-permute-start(bf16[576,384]{1,0:T(8,128)(2,1)S(1)} %left.1.bundle_ref), channel_id=1, source_target_pairs={{0,1},{1,0},{2,3},{3,2},{4,5},{5,4},{6,7},{7,6},{8,9},{9,8},{10,11... | collective-permute-start | bytes 1327112 | tf_op jit(solution)/shard_map/ppermute | solution.py:260

commit v9 on v8

--- a/solution.py
+++ b/solution.py
@@ -44,7 +44,7 @@
     [(zh, xl) for zh in range(4) for xl in range(2)], (2, 0), lambda place: (ring(2 * place[0], 5) + ring(2 * place[0] + 1, 5)) / 2 + place[1]
 )
 COL_ORDER = from_far(
-    [(zl, y) for zl in range(2) for y in range(8)], (1, 4), lambda place: ring(place[1], 4) + 1 - place[0]
+    [(zl, y) for zl in range(2) for y in range(8)], (1, 4), lambda place: ring(place[1], 4) + (1 - place[0]) / 2
 )
 
 

time: 75 us -> 75 us (level)
  waiting for transfers between devices: 12.5 us -> 13.7 us
    ppermute x1, waiting for transfers between devices: 0.54 us -> 1.56 us  [per_device(): cross = lax.ppermute(away, AXES, swap(True, True))]
    all_to_all x1, waiting for transfers between devices: 11.3 us -> 12.1 us  [per_device(): both = exchange(send)]
  transfers between devices with their start and end apart: 4 -> 4, of which waited for: 3 -> 2; matrix products, arithmetic and copies ran while one was open for 0% -> 0% of each run, Pallas kernels for 1% -> 1%
where the time goes in v9:
time: 75 us; the launch traced here: 74.6 us
  starting transfers between devices  31 us (41%)
  blocking collectives  20.4 us (27%)
  waiting for transfers between devices  13.7 us (18%)
  Pallas kernels  7.17 us (10%)
  local copies, waits for them, and re-layouts  2.19 us (3%)
    all_to_all x1, starting transfers between devices, per_device(): both = exchange(send)  21.1 us
    all_to_all x1, blocking collectives, per_device(): combined = exchange(combined)  20.4 us
    all_to_all x1, waiting for transfers between devices, per_device(): both = exchange(send)  12.1 us
    ppermute x1, starting transfers between devices, per_device(): cross = lax.ppermute(away, AXES, swap(True, True))  4.27 us
    ppermute x1, starting transfers between devices, per_device(): mirror = lax.ppermute(keep, AXES, swap(True, False))  3.72 us
    pallas_call x1, Pallas kernels, per_device(): pl.pallas_call(factors_kernel, out_shape=(shape((WIDTH, 2, 2 * SPAN), BF1...  3.23 us
    unnamed x10, local copies, waits for them, and re-layouts  1.96 us
    ppermute x1, starting transfers between devices, per_device(): bundle_core = lax.ppermute(bundle, AXES, swap(False, True))  1.92 us
  transfers between devices with their start and end apart: 4, of which 2 were waited for; matrix products, arithmetic and copies ran while one was open for 0% of the time, Pallas kernels for 1%

profile of v9, /device:TPU:1, one launch (start us, length us, event | category | flops | bytes accessed | tf_op | source)
XLA Modules:
  0.0 74.6 jit_solution(15555142980233552285)
XLA Ops:
  0.0 3.2 %factors.1 = (bf16[128,2,1152]{2,1,0:T(2,128)(2,1)}, bf16[1152,128]{1,0:T(8,128)(2,1)}) custom-call(bf16[1152,128]{1,0:T(8,128)(2,1)} %bitcast.9, s32[24,48]{1,0:T(8,128)} %bitcast.10, f32[1,128]{1,0:T(1,128)} %bitcast.11, f32[1,128]{1,0:T(1,128)} %bitcast.12, bf16[128,512]{1,0:T(8,128)(2,1)} %refs_4_.1), custom_call_target="tpu_custom_call" | custom-call | tf_op jit(solution)/shard_map/factors/pallas_call | solution.py:225
  3.2 0.0 copy-start
  3.3 21.1 %all-to-all-start = ((bf16[128,2,1152]{2,1,0:T(2,128)(2,1)}), bf16[128,2,1152]{2,1,0:T(2,128)(2,1)S(1)}, u32[]{:S(2)}, u32[]{:S(2)}) async-start(bf16[128,2,1152]{2,1,0:T(2,128)(2,1)} %get-tuple-element.18), calls=%async_computation | async-start | bytes 1179648 | tf_op jit(solution)/shard_map/all_to_all | solution.py:244
  24.3 0.0 copy-start.3
  24.3 0.6 copy-done.3
  25.0 0.1 copy.10.rest_refs_0_
  25.1 0.0 copy-start.4
  25.1 0.7 copy-done.4
  25.8 0.0 copy-start.1
  25.8 0.0 copy-start.2
  25.8 0.1 copy.11.rest_refs_1_
  25.9 0.0 copy-done
  25.9 0.6 copy-done.1
  26.5 0.0 copy-done.2
  26.5 0.2 gate.1
  26.8 12.1 %all-to-all-done.x_ref = bf16[128,2,1152]{2,1,0:T(2,128)(2,1)S(1)} async-done(((bf16[128,2,1152]{2,1,0:T(2,128)(2,1)}), bf16[128,2,1152]{2,1,0:T(2,128)(2,1)S(1)}, u32[]{:S(2)}, u32[]{:S(2)}) %all-to-all-start) | async-done | bytes 589856 | tf_op jit(solution)/shard_map/all_to_all | solution.py:244
  38.9 0.5 right.1
  39.4 3.7 %collective-permute-start.2 = (bf16[192,384]{1,0:T(8,128)(2,1)S(1)}, bf16[192,384]{1,0:T(8,128)(2,1)S(1)}, u32[]{:S(2)}, u32[]{:S(2)}) collective-permute-start(bf16[192,384]{1,0:T(8,128)(2,1)S(1)} %get-tuple-element.26.keep_ref), channel_id=1, source_target_pairs={{0,96},{1,97},{2,98},{3,99},{4,100},{5,101},{6,102},{7,103},{8,104... | collective-permute-start | bytes 442376 | tf_op jit(solution)/shard_map/ppermute | solution.py:257
  43.1 4.3 %collective-permute-start.1 = (bf16[192,384]{1,0:T(8,128)(2,1)S(1)}, bf16[192,384]{1,0:T(8,128)(2,1)S(1)}, u32[]{:S(2)}, u32[]{:S(2)}) collective-permute-start(bf16[192,384]{1,0:T(8,128)(2,1)S(1)} %get-tuple-element.19.away_ref), channel_id=1, source_target_pairs={{0,97},{1,96},{2,99},{3,98},{4,101},{5,100},{6,103},{7,102},{8,105... | collective-permute-start | bytes 442376 | tf_op jit(solution)/shard_map/ppermute | solution.py:258
  47.4 0.3 left.1.bundle_ref
  47.7 1.9 %collective-permute-start = (bf16[576,384]{1,0:T(8,128)(2,1)S(1)}, bf16[576,384]{1,0:T(8,128)(2,1)S(1)}, u32[]{:S(2)}, u32[]{:S(2)}) collective-permute-start(bf16[576,384]{1,0:T(8,128)(2,1)S(1)} %left.1.bundle_ref), channel_id=1, source_target_pairs={{0,1},{1,0},{2,3},{3,2},{4,5},{5,4},{6,7},{7,6},{8,9},{9,8},{10,11... | collective-permute-start | bytes 1327112 | tf_op jit(solution)/shard_map/ppermute | solution.py:260
  49.7 0.0 collective-permute-done.2.mirror_ref
  49.7 0.5 own.1.own_ref
  50.2 1.6 %collective-permute-done.1.cross_ref = bf16[192,384]{1,0:T(8,128)(2,1)S(1)} collective-permute-done((bf16[192,384]{1,0:T(8,128)(2,1)S(1)}, bf16[192,384]{1,0:T(8,128)(2,1)S(1)}, u32[]{:S(2)}, u32[]{:S(2)}) %collective-permute-start.1) | collective-permute-done | bytes 147488 | tf_op jit(solution)/shard_map/ppermute | solution.py:258
  51.8 0.0 collective-permute-done.bundle_ref
  51.8 0.8 %contract.1 = bf16[128,2,624]{2,1,0:T(2,128)(2,1)S(1)} custom-call(bf16[576,384]{1,0:T(8,128)(2,1)S(1)} %collective-permute-done.bundle_ref, bf16[192,384]{1,0:T(8,128)(2,1)S(1)} %collective-permute-done.1.cross_ref, f32[3,384,128]{2,1,0:T(8,128)S(1)} %own.1.own_ref, s32[1]{0:T(128)} %bitcast.7.side_ref), custom_call_target="tpu_custom_call" | custom-call | tf_op jit(solution)/shard_map/contract/pallas_call | solution.py:269
  52.6 20.4 %all_to_all.10.x_ref = bf16[128,2,624]{2,1,0:T(2,128)(2,1)S(1)} all-to-all(bf16[128,2,624]{2,1,0:T(2,128)(2,1)S(1)} %contract.1), channel_id=1, replica_groups={{280,256,272,258,270,274,286,260,268,276,284,262,266,278,282,264,56,32,..., dimensions={0} | all-to-all | bytes 638976 | tf_op jit(solution)/shard_map/all_to_all | solution.py:277
  73.1 1.5 %update.1 = bf16[1152,128]{1,0:T(8,128)(2,1)} custom-call(bf16[128,2,624]{2,1,0:T(2,128)(2,1)S(1)} %all_to_all.10.x_ref, f32[1152,128]{1,0:T(8,128)S(1)} %get-tuple-element.27.gate_ref, f32[128,1]{1,0:T(8,128)S(1)} %get-tuple-element.28.gain_ref, f32[128,1]{1,0:T(8,128)S(1)} %get-tuple-element.29.bias_ref, bf16[128,128]{1,0:T(8,128)(2,1)S(1)} %get-tuple-element.30.w_ref), custom_call_target="tpu_custom_call" | custom-call | tf_op jit(solution)/shard_map/update/pallas_call | solution.py:278
Async XLA Ops:
  3.2 22.6 %copy-start = (bf16[1152,128]{1,0:T(8,128)(2,1)S(1)}, bf16[1152,128]{1,0:T(8,128)(2,1)}, u32[]{:S(2)}) copy-start(bf16[1152,128]{1,0:T(8,128)(2,1)} %get-tuple-element.20.normed_ref) | copy-start | bytes 884740
  3.3 35.6 %all-to-all-start = ((bf16[128,2,1152]{2,1,0:T(2,128)(2,1)}), bf16[128,2,1152]{2,1,0:T(2,128)(2,1)S(1)}, u32[]{:S(2)}, u32[]{:S(2)}) async-start(bf16[128,2,1152]{2,1,0:T(2,128)(2,1)} %get-tuple-element.18), calls=%async_computation | async-start | bytes 1179648 | tf_op jit(solution)/shard_map/all_to_all | solution.py:244
  24.3 0.7 copy-start.3
  25.1 0.7 copy-start.4
  25.8 0.8 %copy-start.1 = (bf16[128,128]{1,0:T(8,128)(2,1)S(1)}, bf16[128,128]{1,0:T(8,128)(2,1)}, u32[]{:S(2)}) copy-start(bf16[128,128]{1,0:T(8,128)(2,1)} %w_ref.1) | copy-start | bytes 98308
  25.8 0.8 %copy-start.2 = (bf16[128,128]{1,0:T(8,128)(2,1)S(1)}, bf16[128,128]{1,0:T(8,128)(2,1)}, u32[]{:S(2)}) copy-start(bf16[128,128]{1,0:T(8,128)(2,1)} %rest_refs_2_.1) | copy-start | bytes 98308
  39.4 10.3 %collective-permute-start.2 = (bf16[192,384]{1,0:T(8,128)(2,1)S(1)}, bf16[192,384]{1,0:T(8,128)(2,1)S(1)}, u32[]{:S(2)}, u32[]{:S(2)}) collective-permute-start(bf16[192,384]{1,0:T(8,128)(2,1)S(1)} %get-tuple-element.26.keep_ref), channel_id=1, source_target_pairs={{0,96},{1,97},{2,98},{3,99},{4,100},{5,101},{6,102},{7,103},{8,104... | collective-permute-start | bytes 442376 | tf_op jit(solution)/shard_map/ppermute | solution.py:257
  43.1 8.6 %collective-permute-start.1 = (bf16[192,384]{1,0:T(8,128)(2,1)S(1)}, bf16[192,384]{1,0:T(8,128)(2,1)S(1)}, u32[]{:S(2)}, u32[]{:S(2)}) collective-permute-start(bf16[192,384]{1,0:T(8,128)(2,1)S(1)} %get-tuple-element.19.away_ref), channel_id=1, source_target_pairs={{0,97},{1,96},{2,99},{3,98},{4,101},{5,100},{6,103},{7,102},{8,105... | collective-permute-start | bytes 442376 | tf_op jit(solution)/shard_map/ppermute | solution.py:258
  47.7 4.1 %collective-permute-start = (bf16[576,384]{1,0:T(8,128)(2,1)S(1)}, bf16[576,384]{1,0:T(8,128)(2,1)S(1)}, u32[]{:S(2)}, u32[]{:S(2)}) collective-permute-start(bf16[576,384]{1,0:T(8,128)(2,1)S(1)} %left.1.bundle_ref), channel_id=1, source_target_pairs={{0,1},{1,0},{2,3},{3,2},{4,5},{5,4},{6,7},{7,6},{8,9},{9,8},{10,11... | collective-permute-start | bytes 1327112 | tf_op jit(solution)/shard_map/ppermute | solution.py:260

commit v10 on v9

--- a/solution.py
+++ b/solution.py
@@ -41,7 +41,7 @@
 
 
 ROW_ORDER = from_far(
-    [(zh, xl) for zh in range(4) for xl in range(2)], (2, 0), lambda place: (ring(2 * place[0], 5) + ring(2 * place[0] + 1, 5)) / 2 + place[1]
+    [(zh, xl) for zh in range(4) for xl in range(2)], (2, 0), lambda place: (ring(2 * place[0], 5) + ring(2 * place[0] + 1, 5)) / 2 - place[1] / 4
 )
 COL_ORDER = from_far(
     [(zl, y) for zl in range(2) for y in range(8)], (1, 4), lambda place: ring(place[1], 4) + (1 - place[0]) / 2

time: 75 us -> 75.9 us (1.012)
  waiting for transfers between devices: 13.7 us -> 12.8 us
  starting transfers between devices: 31 us -> 31.8 us
    ppermute x1, waiting for transfers between devices: 1.56 us -> 0.31 us  [per_device(): cross = lax.ppermute(away, AXES, swap(True, True))]
    ppermute x1, waiting for transfers between devices: 0.01 us -> 0.89 us  [per_device(): bundle_core = lax.ppermute(bundle, AXES, swap(False, True))]
    ppermute x1, starting transfers between devices: 4.27 us -> 5.15 us  [per_device(): cross = lax.ppermute(away, AXES, swap(True, True))]
  transfers between devices with their start and end apart: 4 -> 4, of which waited for: 2 -> 3; matrix products, arithmetic and copies ran while one was open for 0% -> 0% of each run, Pallas kernels for 1% -> 1%
where the time goes in v10:
time: 75.9 us; the launch traced here: 75 us
  starting transfers between devices  31.8 us (42%)
  blocking collectives  20.9 us (28%)
  waiting for transfers between devices  12.8 us (17%)
  Pallas kernels  7.17 us (9%)
  local copies, waits for them, and re-layouts  2.19 us (3%)
    all_to_all x1, starting transfers between devices, per_device(): both = exchange(send)  21 us
    all_to_all x1, blocking collectives, per_device(): combined = exchange(combined)  20.9 us
    all_to_all x1, waiting for transfers between devices, per_device(): both = exchange(send)  11.6 us
    ppermute x1, starting transfers between devices, per_device(): cross = lax.ppermute(away, AXES, swap(True, True))  5.15 us
    ppermute x1, starting transfers between devices, per_device(): mirror = lax.ppermute(keep, AXES, swap(True, False))  3.72 us
    pallas_call x1, Pallas kernels, per_device(): pl.pallas_call(factors_kernel, out_shape=(shape((WIDTH, 2, 2 * SPAN), BF1...  3.23 us
    unnamed x10, local copies, waits for them, and re-layouts  1.96 us
    ppermute x1, starting transfers between devices, per_device(): bundle_core = lax.ppermute(bundle, AXES, swap(False, True))  1.92 us
  transfers between devices with their start and end apart: 4, of which 3 were waited for; matrix products, arithmetic and copies ran while one was open for 0% of the time, Pallas kernels for 1%

profile of v10, /device:TPU:1, one launch (start us, length us, event | category | flops | bytes accessed | tf_op | source)
XLA Modules:
  0.0 75.0 jit_solution(3881862327376477039)
XLA Ops:
  0.0 3.2 %factors.1 = (bf16[128,2,1152]{2,1,0:T(2,128)(2,1)}, bf16[1152,128]{1,0:T(8,128)(2,1)}) custom-call(bf16[1152,128]{1,0:T(8,128)(2,1)} %bitcast.9, s32[24,48]{1,0:T(8,128)} %bitcast.10, f32[1,128]{1,0:T(1,128)} %bitcast.11, f32[1,128]{1,0:T(1,128)} %bitcast.12, bf16[128,512]{1,0:T(8,128)(2,1)} %refs_4_.1), custom_call_target="tpu_custom_call" | custom-call | tf_op jit(solution)/shard_map/factors/pallas_call | solution.py:225
  3.2 0.0 copy-start
  3.3 21.0 %all-to-all-start = ((bf16[128,2,1152]{2,1,0:T(2,128)(2,1)}), bf16[128,2,1152]{2,1,0:T(2,128)(2,1)S(1)}, u32[]{:S(2)}, u32[]{:S(2)}) async-start(bf16[128,2,1152]{2,1,0:T(2,128)(2,1)} %get-tuple-element.18), calls=%async_computation | async-start | bytes 1179648 | tf_op jit(solution)/shard_map/all_to_all | solution.py:244
  24.2 0.0 copy-start.3
  24.2 0.6 copy-done.3
  24.9 0.1 copy.10.rest_refs_0_
  25.0 0.0 copy-start.4
  25.0 0.7 copy-done.4
  25.7 0.0 copy-start.1
  25.7 0.0 copy-start.2
  25.7 0.1 copy.11.rest_refs_1_
  25.8 0.0 copy-done
  25.8 0.6 copy-done.1
  26.4 0.0 copy-done.2
  26.4 0.2 gate.1
  26.7 11.6 %all-to-all-done.x_ref = bf16[128,2,1152]{2,1,0:T(2,128)(2,1)S(1)} async-done(((bf16[128,2,1152]{2,1,0:T(2,128)(2,1)}), bf16[128,2,1152]{2,1,0:T(2,128)(2,1)S(1)}, u32[]{:S(2)}, u32[]{:S(2)}) %all-to-all-start) | async-done | bytes 589856 | tf_op jit(solution)/shard_map/all_to_all | solution.py:244
  38.3 0.5 right.1
  38.8 3.7 %collective-permute-start.2 = (bf16[192,384]{1,0:T(8,128)(2,1)S(1)}, bf16[192,384]{1,0:T(8,128)(2,1)S(1)}, u32[]{:S(2)}, u32[]{:S(2)}) collective-permute-start(bf16[192,384]{1,0:T(8,128)(2,1)S(1)} %get-tuple-element.26.keep_ref), channel_id=1, source_target_pairs={{0,96},{1,97},{2,98},{3,99},{4,100},{5,101},{6,102},{7,103},{8,104... | collective-permute-start | bytes 442376 | tf_op jit(solution)/shard_map/ppermute | solution.py:257
  42.5 5.2 %collective-permute-start.1 = (bf16[192,384]{1,0:T(8,128)(2,1)S(1)}, bf16[192,384]{1,0:T(8,128)(2,1)S(1)}, u32[]{:S(2)}, u32[]{:S(2)}) collective-permute-start(bf16[192,384]{1,0:T(8,128)(2,1)S(1)} %get-tuple-element.19.away_ref), channel_id=1, source_target_pairs={{0,97},{1,96},{2,99},{3,98},{4,101},{5,100},{6,103},{7,102},{8,105... | collective-permute-start | bytes 442376 | tf_op jit(solution)/shard_map/ppermute | solution.py:258
  47.7 0.3 left.1.bundle_ref
  48.0 1.9 %collective-permute-start = (bf16[576,384]{1,0:T(8,128)(2,1)S(1)}, bf16[576,384]{1,0:T(8,128)(2,1)S(1)}, u32[]{:S(2)}, u32[]{:S(2)}) collective-permute-start(bf16[576,384]{1,0:T(8,128)(2,1)S(1)} %left.1.bundle_ref), channel_id=1, source_target_pairs={{0,1},{1,0},{2,3},{3,2},{4,5},{5,4},{6,7},{7,6},{8,9},{9,8},{10,11... | collective-permute-start | bytes 1327112 | tf_op jit(solution)/shard_map/ppermute | solution.py:260
  49.9 0.0 collective-permute-done.2.mirror_ref
  50.0 0.5 own.1.own_ref
  50.5 0.3 collective-permute-done.1.cross_ref
  50.8 0.9 %collective-permute-done.bundle_ref = bf16[576,384]{1,0:T(8,128)(2,1)S(1)} collective-permute-done((bf16[576,384]{1,0:T(8,128)(2,1)S(1)}, bf16[576,384]{1,0:T(8,128)(2,1)S(1)}, u32[]{:S(2)}, u32[]{:S(2)}) %collective-permute-start) | collective-permute-done | bytes 442400 | tf_op jit(solution)/shard_map/ppermute | solution.py:260
  51.7 0.8 %contract.1 = bf16[128,2,624]{2,1,0:T(2,128)(2,1)S(1)} custom-call(bf16[576,384]{1,0:T(8,128)(2,1)S(1)} %collective-permute-done.bundle_ref, bf16[192,384]{1,0:T(8,128)(2,1)S(1)} %collective-permute-done.1.cross_ref, f32[3,384,128]{2,1,0:T(8,128)S(1)} %own.1.own_ref, s32[1]{0:T(128)} %bitcast.7.side_ref), custom_call_target="tpu_custom_call" | custom-call | tf_op jit(solution)/shard_map/contract/pallas_call | solution.py:269
  52.5 20.9 %all_to_all.10.x_ref = bf16[128,2,624]{2,1,0:T(2,128)(2,1)S(1)} all-to-all(bf16[128,2,624]{2,1,0:T(2,128)(2,1)S(1)} %contract.1), channel_id=1, replica_groups={{280,256,272,258,270,274,286,260,268,276,284,262,266,278,282,264,24,0,1..., dimensions={0} | all-to-all | bytes 638976 | tf_op jit(solution)/shard_map/all_to_all | solution.py:277
  73.5 1.5 %update.1 = bf16[1152,128]{1,0:T(8,128)(2,1)} custom-call(bf16[128,2,624]{2,1,0:T(2,128)(2,1)S(1)} %all_to_all.10.x_ref, f32[1152,128]{1,0:T(8,128)S(1)} %get-tuple-element.27.gate_ref, f32[128,1]{1,0:T(8,128)S(1)} %get-tuple-element.28.gain_ref, f32[128,1]{1,0:T(8,128)S(1)} %get-tuple-element.29.bias_ref, bf16[128,128]{1,0:T(8,128)(2,1)S(1)} %get-tuple-element.30.w_ref), custom_call_target="tpu_custom_call" | custom-call | tf_op jit(solution)/shard_map/update/pallas_call | solution.py:278
Async XLA Ops:
  3.2 22.5 %copy-start = (bf16[1152,128]{1,0:T(8,128)(2,1)S(1)}, bf16[1152,128]{1,0:T(8,128)(2,1)}, u32[]{:S(2)}) copy-start(bf16[1152,128]{1,0:T(8,128)(2,1)} %get-tuple-element.20.normed_ref) | copy-start | bytes 884740
  3.3 35.0 %all-to-all-start = ((bf16[128,2,1152]{2,1,0:T(2,128)(2,1)}), bf16[128,2,1152]{2,1,0:T(2,128)(2,1)S(1)}, u32[]{:S(2)}, u32[]{:S(2)}) async-start(bf16[128,2,1152]{2,1,0:T(2,128)(2,1)} %get-tuple-element.18), calls=%async_computation | async-start | bytes 1179648 | tf_op jit(solution)/shard_map/all_to_all | solution.py:244
  24.2 0.7 copy-start.3
  25.0 0.7 copy-start.4
  25.7 0.8 %copy-start.1 = (bf16[128,128]{1,0:T(8,128)(2,1)S(1)}, bf16[128,128]{1,0:T(8,128)(2,1)}, u32[]{:S(2)}) copy-start(bf16[128,128]{1,0:T(8,128)(2,1)} %w_ref.1) | copy-start | bytes 98308
  25.7 0.8 %copy-start.2 = (bf16[128,128]{1,0:T(8,128)(2,1)S(1)}, bf16[128,128]{1,0:T(8,128)(2,1)}, u32[]{:S(2)}) copy-start(bf16[128,128]{1,0:T(8,128)(2,1)} %rest_refs_2_.1) | copy-start | bytes 98308
  38.8 11.2 %collective-permute-start.2 = (bf16[192,384]{1,0:T(8,128)(2,1)S(1)}, bf16[192,384]{1,0:T(8,128)(2,1)S(1)}, u32[]{:S(2)}, u32[]{:S(2)}) collective-permute-start(bf16[192,384]{1,0:T(8,128)(2,1)S(1)} %get-tuple-element.26.keep_ref), channel_id=1, source_target_pairs={{0,96},{1,97},{2,98},{3,99},{4,100},{5,101},{6,102},{7,103},{8,104... | collective-permute-start | bytes 442376 | tf_op jit(solution)/shard_map/ppermute | solution.py:257
  42.5 8.3 %collective-permute-start.1 = (bf16[192,384]{1,0:T(8,128)(2,1)S(1)}, bf16[192,384]{1,0:T(8,128)(2,1)S(1)}, u32[]{:S(2)}, u32[]{:S(2)}) collective-permute-start(bf16[192,384]{1,0:T(8,128)(2,1)S(1)} %get-tuple-element.19.away_ref), channel_id=1, source_target_pairs={{0,97},{1,96},{2,99},{3,98},{4,101},{5,100},{6,103},{7,102},{8,105... | collective-permute-start | bytes 442376 | tf_op jit(solution)/shard_map/ppermute | solution.py:258
  48.0 3.7 %collective-permute-start = (bf16[576,384]{1,0:T(8,128)(2,1)S(1)}, bf16[576,384]{1,0:T(8,128)(2,1)S(1)}, u32[]{:S(2)}, u32[]{:S(2)}) collective-permute-start(bf16[576,384]{1,0:T(8,128)(2,1)S(1)} %left.1.bundle_ref), channel_id=1, source_target_pairs={{0,1},{1,0},{2,3},{3,2},{4,5},{5,4},{6,7},{7,6},{8,9},{9,8},{10,11... | collective-permute-start | bytes 1327112 | tf_op jit(solution)/shard_map/ppermute | solution.py:260
